TPU v7x, 256 devices: a whole 4x4x8 slice. The times are simulated.
256 devices in a mesh: dp: 4 (over x), seq: 64 (over z, y, core).
Axes of the slice: x: 4, y: 4, z: 8, core: 2. Of those that a mesh axis runs over, the one named last changes fastest.
Arguments:
- latents: bfloat16 [4, 64, 256, 1152], P('dp', 'seq'), may hold values from -16 to 16
- in_weight: bfloat16 [1152, 3456], replicated
- out_weight: bfloat16 [1152, 1152], replicated, may hold values from -0.1875 to 0.1875
- cotangent: bfloat16 [4, 64, 256, 1152], P('dp', 'seq'), may hold values from -6 to 6
- clip_lengths: int32 [4, 4], P('dp'), may hold values from 1 to 32, 64 in all within a row
Outputs:
- mixed: bfloat16 [4, 64, 256, 1152], P('dp', 'seq')
- grad_latents: bfloat16 [4, 64, 256, 1152], P('dp', 'seq')
- out_grad: float32 [1152, 1152], P('seq')
Inputs may be any that keep to these rules, and one draw needn't show every extreme that they name: `clip_lengths`: the 4 lengths of a sequence sum to 64; in every sequence the longest is exactly 32.
All inputs are finite; a program needn't handle non-finite values.
Results may differ from a plain program's by a relative error of at most 0.013.
The roundings to bfloat16 on the way count: a program that leaves them out, or rounds other values in their place, can miss the bound.
Values may be sent and summed in bfloat16 or wider, within the bound.
A program may use at most 128 MiB of HBM per device.

v0:
```python
import jax
import jax.numpy as jnp
from jax import lax
from jax.sharding import PartitionSpec as P

HEADS = 16
HD = 72


def clip_index(lengths, frames):
    ends = jnp.cumsum(lengths)
    position = jnp.arange(frames, dtype=jnp.int32)
    return jnp.sum((ends[None, :] <= position[:, None]).astype(jnp.int32), axis=1)


def softmax_weights(query, key_rows, same):
    scale = 1.0 / jnp.sqrt(jnp.float32(HD))
    scores = (
        jnp.einsum("fphd,gphd->phfg", query, key_rows, preferred_element_type=jnp.float32) * scale
    )
    scores = jnp.where(same[None, None], scores, -jnp.inf)
    return jax.nn.softmax(scores, axis=-1)


def contract_rows(left, right):
    return lax.dot_general(
        left, right, (((0,), (0,)), ((), ())), preferred_element_type=jnp.float32
    )


def contract_cols(left, right):
    return lax.dot_general(
        left, right, (((1,), (1,)), ((), ())), preferred_element_type=jnp.float32
    )


def body(latents, in_weight, out_weight, cotangent, clip_lengths):
    shards = lax.axis_size("seq")
    local_frames = latents.shape[1]
    patches = latents.shape[2]
    width = latents.shape[3]
    frames = local_frames * shards
    local_patches = patches // shards
    inner = HEADS * HD
    tok_rows = latents.reshape(local_frames * patches, width)
    projected = jnp.dot(tok_rows, in_weight, preferred_element_type=jnp.float32).astype(
        jnp.bfloat16
    )
    projected = projected.reshape(1, local_frames, patches, 3 * inner)
    patch_proj = lax.all_to_all(projected, "seq", split_axis=2, concat_axis=1, tiled=True)
    split = patch_proj.reshape(frames, local_patches, 3, HEADS, HD)
    query, key_rows, value_rows = (split[:, :, 0], split[:, :, 1], split[:, :, 2])
    clip = clip_index(clip_lengths[0], frames)
    same = clip[:, None] == clip[None, :]
    weights32 = softmax_weights(query, key_rows, same)
    weights = weights32.astype(jnp.bfloat16)
    attended = jnp.einsum(
        "phfg,gphd->fphd", weights, value_rows, preferred_element_type=jnp.float32
    ).astype(jnp.bfloat16)
    attended = attended.reshape(1, frames, local_patches, inner)
    frame_att = lax.all_to_all(attended, "seq", split_axis=1, concat_axis=2, tiled=True)
    att_rows = frame_att.reshape(local_frames * patches, inner)
    mixed = jnp.dot(att_rows, out_weight, preferred_element_type=jnp.float32).astype(jnp.bfloat16)
    cot_rows = cotangent.reshape(local_frames * patches, width)
    grad_att = contract_cols(cot_rows, out_weight).astype(jnp.bfloat16)
    grad_att = grad_att.reshape(1, local_frames, patches, inner)
    patch_grad_att = lax.all_to_all(grad_att, "seq", split_axis=2, concat_axis=1, tiled=True)
    out_part = lax.psum_scatter(
        contract_rows(att_rows, cot_rows), "seq", scatter_dimension=0, tiled=True
    )
    grad_heads = patch_grad_att.reshape(frames, local_patches, HEADS, HD)
    grad_weights = jnp.einsum(
        "fphd,gphd->phfg", grad_heads, value_rows, preferred_element_type=jnp.float32
    )
    grad_values = jnp.einsum(
        "phfg,fphd->gphd", weights, grad_heads, preferred_element_type=jnp.float32
    ).astype(jnp.bfloat16)
    totals = jnp.sum(weights32 * grad_weights, axis=-1, keepdims=True)
    scale = 1.0 / jnp.sqrt(jnp.float32(HD))
    grad_scores = (weights32 * (grad_weights - totals) * scale).astype(jnp.bfloat16)
    grad_query = jnp.einsum(
        "phfg,gphd->fphd", grad_scores, key_rows, preferred_element_type=jnp.float32
    ).astype(jnp.bfloat16)
    grad_keys = jnp.einsum(
        "phfg,fphd->gphd", grad_scores, query, preferred_element_type=jnp.float32
    ).astype(jnp.bfloat16)
    grad_proj = jnp.stack([grad_query, grad_keys, grad_values], axis=2)
    grad_proj = grad_proj.reshape(1, frames, local_patches, 3 * inner)
    frame_grad = lax.all_to_all(grad_proj, "seq", split_axis=1, concat_axis=2, tiled=True)
    grad_rows = frame_grad.reshape(local_frames * patches, 3 * inner)
    grad_latents = contract_cols(grad_rows, in_weight).astype(jnp.bfloat16).reshape(latents.shape)
    out_grad = lax.psum(out_part.astype(jnp.bfloat16), "dp").astype(jnp.float32)
    return (mixed.reshape(latents.shape), grad_latents, out_grad)


def solution(mesh):
    placed = (P("dp", "seq", None, None), P(), P(), P("dp", "seq", None, None), P("dp", None))
    return jax.shard_map(
        body,
        mesh=mesh,
        in_specs=placed,
        out_specs=(P("dp", "seq", None, None), P("dp", "seq", None, None), P("seq", None)),
        check_vma=False,
    )
```

profile of v0, /device:TPU:128, one launch (start us, length us, event | category | flops | bytes accessed | tf_op | source)
XLA Modules:
  0.0 563.4 jit_solution(589383938545123805)
XLA Ops:
  6.9 5.2 reduce.5
  13.3 10.8 %all-to-all-start.2 = ((bf16[64,2,2304]{2,1,0:T(2,128)(2,1)}), bf16[64,2,2304]{2,1,0:T(2,128)(2,1)S(1)}, u32[]{:S(2)}, u32[]{:S(2)}) async-start(bf16[64,2,2304]{2,1,0:T(2,128)(2,1)} %reshape.133), calls=%async_computation.2 | async-start | bytes 1179648 | tf_op jit(solution)/shard_map/all_to_all | solution.py:67
  24.1 6.0 %fusion.2 = bf16[1,1,256,3456]{3,2,1,0:T(8,128)(2,1)S(1)} fusion(bf16[1152,3456]{1,0:T(8,128)(2,1)} %param.6, bf16[1,1,256,1152]{3,2,1,0:T(8,128)(2,1)} %param.5), kind=kOutput, calls=%fused_computation.3 | convolution fusion | flops 2039316480 | bytes 10321920 | tf_op jit(solution)/shard_map/dot_general | solution.py:46
  30.1 4.5 copy.109
  34.6 13.0 %reduce.4 = bf16[256,3456]{1,0:T(8,128)(2,1)} reduce(bf16[256,1,1,3456]{3,2,1,0:T(2,128)(2,1)} %bitcast.86, bf16[]{:T(256)} %broadcast.43), dimensions={1,2}, to_apply=%bitcast.84.reduce_sub_computation | reduce | bytes 3538946
  47.6 4.8 reshape.131
  52.5 11.0 %all-to-all-start = ((bf16[64,2,6912]{2,1,0:T(2,128)(2,1)}), bf16[64,2,6912]{2,1,0:T(2,128)(2,1)}, u32[]{:S(2)}, u32[]{:S(2)}) async-start(bf16[64,2,6912]{2,1,0:T(2,128)(2,1)} %reshape.131), calls=%async_computation | async-start | bytes 3538944 | tf_op jit(solution)/shard_map/all_to_all | solution.py:50
  66.9 4.7 bitcast_reduce_fusion.1
  74.5 29.4 %all-to-all-done = bf16[64,2,6912]{2,1,0:T(2,128)(2,1)} async-done(((bf16[64,2,6912]{2,1,0:T(2,128)(2,1)}), bf16[64,2,6912]{2,1,0:T(2,128)(2,1)}, u32[]{:S(2)}, u32[]{:S(2)}) %all-to-all-start) | async-done | bytes 1769504 | tf_op jit(solution)/shard_map/all_to_all | solution.py:50
  103.8 10.7 %reshape.132 = bf16[256,1,1,3456]{3,2,1,0:T(2,128)(2,1)} reshape(bf16[64,2,6912]{2,1,0:T(2,128)(2,1)} %all-to-all-done) | data formatting | bytes 3538944
  114.5 12.9 %bitcast_reduce_fusion = bf16[256,3456]{1,0:T(8,128)(2,1)} fusion(bf16[256,1,1,3456]{3,2,1,0:T(2,128)(2,1)} %reshape.132), kind=kLoop, calls=%fused_computation.58 | loop fusion | bytes 3538944 | tf_op jit(solution)/shard_map/all_to_all | solution.py:50
  127.5 8.1 %reshape.114 = bf16[64,4,3,16,72]{4,3,2,1,0:T(8,128)(2,1)} reshape(bf16[256,3456]{1,0:T(8,128)(2,1)} %bitcast_reduce_fusion) | data formatting | bytes 3538944 | tf_op jit(solution)/shard_map/reshape | solution.py:51
  139.5 4.8 fusion.52
  152.8 9.4 %all-to-all-start.1 = ((bf16[1,64,4,1152]{3,2,0,1:T(4,128)(2,1)}), bf16[1,64,4,1152]{3,2,0,1:T(4,128)(2,1)S(1)}, u32[]{:S(2)}, u32[]{:S(2)}) async-start(bf16[1,64,4,1152]{3,2,0,1:T(4,128)(2,1)} %reshape.126), calls=%async_computation.1 | async-start | bytes 1179648 | tf_op jit(solution)/shard_map/all_to_all | solution.py:61
  162.2 4.2 fusion.35
  166.3 6.2 %fusion.27 = bf16[64,4,1,16,72]{4,0,3,1,2:T(8,128)(2,1)} fusion(f32[4,16,64,64]{2,3,1,0:T(8,128)} %fusion.35, bf16[64,4,1,16,72]{4,3,2,1,0:T(8,128)(2,1)} %get-tuple-element.3, f32[4,16,64,64]{2,3,1,0:T(8,128)} %get-tuple-element.7, f32[4,16,64]{2,1,0:T(8,128)S(1)} %get-tuple-element.6), kind=kOutput, calls=%fused_computation.26 | convolution fusion | flops 39882816 | bytes 3293184 | tf_op jit(solution)/shard_map/phfg,gphd->fphd/dot_general | solution.py:81
  172.5 6.4 %fusion.24 = bf16[64,4,1,16,72]{4,0,3,1,2:T(8,128)(2,1)} fusion(f32[4,16,64,64]{2,3,1,0:T(8,128)} %fusion.35, bf16[64,4,1,16,72]{4,3,2,1,0:T(8,128)(2,1)} %get-tuple-element.4, f32[4,16,64,64]{2,3,1,0:T(8,128)} %get-tuple-element.7, f32[4,16,64]{2,1,0:T(8,128)S(1)} %get-tuple-element.6), kind=kOutput, calls=%fused_computation.25 | convolution fusion | flops 39882816 | bytes 3293184 | tf_op jit(solution)/shard_map/phfg,fphd->gphd/dot_general | solution.py:84
  186.6 7.6 %reshape.127 = bf16[1,64,4,3456]{3,2,0,1:T(4,128)(2,1)} reshape(bf16[64,4,3,16,72]{4,3,2,1,0:T(8,128)(2,1)} %copy.72) | data formatting | bytes 3538944 | tf_op jit(solution)/shard_map/reshape | solution.py:88
  195.0 10.9 %all-to-all-start.3 = ((bf16[1,64,4,3456]{3,2,0,1:T(4,128)(2,1)}), bf16[1,64,4,3456]{3,2,0,1:T(4,128)(2,1)}, u32[]{:S(2)}, u32[]{:S(2)}) async-start(bf16[1,64,4,3456]{3,2,0,1:T(4,128)(2,1)} %reshape.127), calls=%async_computation.3 | async-start | bytes 3538944 | tf_op jit(solution)/shard_map/all_to_all | solution.py:89
  207.3 4.4 fusion.39
  211.7 319.5 %all-reduce.2 = bf16[1152,1152]{1,0:T(8,128)(2,1)} all-reduce(f32[1152,1152]{1,0:T(8,128)} %fusion.39), channel_id=2, replica_groups=mesh['dp'=4,'seq'=64] {'seq'}, use_global_device_ids=true, to_apply=%region_5.6.clone | all-reduce | flops 1327104 | bytes 7962624
  532.1 17.5 %psum.7 = bf16[18,1152]{1,0:T(8,128)(2,1)S(1)} all-reduce(bf16[18,1152]{1,0:T(8,128)(2,1)S(1)} %dynamic-slice_convert_fusion), channel_id=1, replica_groups=mesh['dp'=4,'seq'=64] {'dp'}, use_global_device_ids=true, to_apply=%region_6.7 | all-reduce | flops 20736 | bytes 82944 | tf_op jit(solution)/shard_map/psum | solution.py:92
  552.1 3.9 reshape.124
  556.0 7.2 %fusion.3 = bf16[1,1,256,1152]{3,2,1,0:T(8,128)(2,1)} fusion(bf16[256,3456]{1,0:T(8,128)(2,1)} %reshape.124, bf16[1152,3456]{1,0:T(8,128)(2,1)} %param.6), kind=kOutput, calls=%fused_computation.8 | convolution fusion | flops 2038726656 | bytes 10321920 | tf_op jit(solution)/shard_map/dot_general | solution.py:32
  (36 shorter events, 38.6 us)
Async XLA Ops:
  0.6 1.8 copy-start
  13.3 39.2 %all-to-all-start.2 = ((bf16[64,2,2304]{2,1,0:T(2,128)(2,1)}), bf16[64,2,2304]{2,1,0:T(2,128)(2,1)S(1)}, u32[]{:S(2)}, u32[]{:S(2)}) async-start(bf16[64,2,2304]{2,1,0:T(2,128)(2,1)} %reshape.133), calls=%async_computation.2 | async-start | bytes 1179648 | tf_op jit(solution)/shard_map/all_to_all | solution.py:67
  52.5 11.1 %copy-start.4 = (s32[1,4]{1,0:T(1,128)S(1)}, s32[1,4]{1,0:T(1,128)}, u32[]{:S(2)}) copy-start(s32[1,4]{1,0:T(1,128)} %param.9) | copy-start | bytes 52
  52.5 11.2 %copy-start.5 = (u32[256]{0:T(256)S(1)}, u32[256]{0:T(256)}, u32[]{:S(2)}) copy-start(u32[256]{0:T(256)} %constant.17) | copy-start | bytes 3076
  52.5 51.3 %all-to-all-start = ((bf16[64,2,6912]{2,1,0:T(2,128)(2,1)}), bf16[64,2,6912]{2,1,0:T(2,128)(2,1)}, u32[]{:S(2)}, u32[]{:S(2)}) async-start(bf16[64,2,6912]{2,1,0:T(2,128)(2,1)} %reshape.131), calls=%async_computation | async-start | bytes 3538944 | tf_op jit(solution)/shard_map/all_to_all | solution.py:50
  152.8 41.4 %all-to-all-start.1 = ((bf16[1,64,4,1152]{3,2,0,1:T(4,128)(2,1)}), bf16[1,64,4,1152]{3,2,0,1:T(4,128)(2,1)S(1)}, u32[]{:S(2)}, u32[]{:S(2)}) async-start(bf16[1,64,4,1152]{3,2,0,1:T(4,128)(2,1)} %reshape.126), calls=%async_computation.1 | async-start | bytes 1179648 | tf_op jit(solution)/shard_map/all_to_all | solution.py:61
  178.9 3.2 copy-start.2
  178.9 3.2 copy-start.3
  194.2 0.8 copy-start.1
  195.0 357.1 %all-to-all-start.3 = ((bf16[1,64,4,3456]{3,2,0,1:T(4,128)(2,1)}), bf16[1,64,4,3456]{3,2,0,1:T(4,128)(2,1)}, u32[]{:S(2)}, u32[]{:S(2)}) async-start(bf16[1,64,4,3456]{3,2,0,1:T(4,128)(2,1)} %reshape.127), calls=%async_computation.3 | async-start | bytes 3538944 | tf_op jit(solution)/shard_map/all_to_all | solution.py:89
where the time goes:
time: 570 us; the launch traced here: 563 us
  blocking collectives  337 us (59%)
  local copies, waits for them, and re-layouts  83.9 us (15%)
  matrix products  49.4 us (9%)
  starting transfers between devices  42.1 us (7%)
  waiting for transfers between devices  29.4 us (5%)
  other arithmetic  20 us (4%)
    unnamed x1, blocking collectives  319 us
    all_to_all x1, waiting for transfers between devices, body(): lax.all_to_all(projected, 'seq', split_axis=2, concat_axis=1, tiled=True)  29.4 us
    unnamed x18, local copies, waits for them, and re-layouts  22.2 us
    unnamed x2, other arithmetic  18.2 us
    psum x1, blocking collectives, body(): out_grad = lax.psum(out_part.astype(jnp.bfloat16), 'dp').astype(jnp.float32)  17.5 us
    all_to_all x1, local copies, waits for them, and re-layouts, body(): lax.all_to_all(projected, 'seq', split_axis=2, concat_axis=1, tiled=True)  12.9 us
  transfers between devices with their start and end apart: 4, of which 1 were waited for; matrix products, arithmetic and copies ran while one was open for 14% of the time, Pallas kernels for 0%

commit v1 on v0

v1 whole, which is shorter than its diff:
```python
import functools

import jax
import jax.numpy as jnp
from jax import lax
from jax.experimental import pallas as pl
from jax.experimental.pallas import tpu as pltpu
from jax.sharding import PartitionSpec as P

MESH = pl.DeviceIdType.MESH
BF16 = jnp.bfloat16
F32 = jnp.float32
HEADS, HD = 16, 72
INNER = HEADS * HD
ZS, YS, CS, XS = 8, 4, 2, 4
SEQ = ZS * YS * CS
SCALE = float(HD) ** -0.5
NT = (((1,), (1,)), ((), ()))
NN = (((1,), (0,)), ((), ()))
TN = (((0,), (0,)), ((), ()))


def dot(a, b, dims=NN):
    return lax.dot_general(a, b, dims, preferred_element_type=F32)


def window(h):
    lo = h * HD // 128 * 128
    hi = -(-(h * HD + HD) // 128) * 128
    return lo, hi


def lane_mask(h, lo, hi, dtype):
    lane = lax.broadcasted_iota(jnp.int32, (1, hi - lo), 1) + lo
    return ((lane >= h * HD) & (lane < h * HD + HD)).astype(dtype)


class Columns:
    def __init__(self, ref, rows, base):
        self.ref, self.rows, self.base, self.cur = ref, rows, base, None

    def add(self, h, out, lo, hi):
        for t in range(lo, hi, 128):
            part = out[:, t - lo : t - lo + 128]
            if t >= h * HD:
                self.cur = part
            else:
                lane = lax.broadcasted_iota(jnp.int32, (1, 128), 1) + t
                self.cur = jnp.where(lane >= h * HD, part, self.cur)
            if t + 128 <= h * HD + HD:
                self.ref[self.rows, self.base + t : self.base + t + 128] = self.cur.astype(BF16)


def kernel(
    lat_ref, cot_ref, len_ref, inw_hbm, outw_hbm,
    mixed_o, glat_o, og_o,
    xs, xr, cs, cr, ms, gs, inw, outw, qkv, w32s, att, cp, ga, gp, attT, paT, pc,
    gsend, gxr, gown, ysend, yr, zsend, zr, ogs, ogr, amask,
    wsem, lsem, ssem, rsem, psem_s, psem_r, xsem_s, xsem_r, ysem_s, ysem_r, zsem_s, zsem_r, bsem_s, bsem_r,
):
    x = lax.axis_index("dp")
    me = lax.axis_index("seq")
    z, y, c = me // (YS * CS), me // CS % YS, me % CS

    w_in = pltpu.make_async_copy(inw_hbm, inw, wsem.at[0])
    w_out = pltpu.make_async_copy(outw_hbm, outw, wsem.at[1])
    w_in.start()
    w_out.start()

    def peer(j):
        i, r = j // 8, 7 - j % 8
        dz = 4 + i // 2 - i % 2 * i
        return (z + dz) % ZS * (YS * CS) + (y + r // CS) % YS * CS + (c + r) % CS

    barrier = pltpu.get_barrier_semaphore()

    @pl.loop(0, SEQ - 1)
    def _(j):
        pl.semaphore_signal(barrier, inc=1, device_id=(x, peer(j)), device_id_type=MESH)

    for dx in range(1, XS):
        for dc in range(CS):
            pl.semaphore_signal(
                barrier, inc=1, device_id=((x + dx) % XS, z * 8 + y * 2 + (c + dc) % CS), device_id_type=MESH
            )

    xs[...] = lat_ref[...].reshape(SEQ, 4, INNER)
    pl.semaphore_wait(barrier, SEQ - 1 + (XS - 1) * CS)

    def exchange(k, src, dst):
        @pl.loop(0, SEQ - 1)
        def _(j):
            d = peer(j)
            pltpu.make_async_remote_copy(
                src_ref=src.at[d], dst_ref=dst.at[me], send_sem=ssem.at[k], recv_sem=rsem.at[k],
                device_id=(x, d), device_id_type=MESH,
            ).start()

        pltpu.make_async_copy(src.at[me], dst.at[me], lsem.at[k]).start()

    def arrived(k, src, dst):
        pltpu.make_async_copy(src.at[me], dst.at[me], lsem.at[k]).wait()
        part = dst.at[pl.ds(0, SEQ - 1)]
        pltpu.make_async_copy(part, part, rsem.at[k]).wait()

    def sent(k, src):
        part = src.at[pl.ds(0, SEQ - 1)]
        pltpu.make_async_copy(part, part, ssem.at[k]).wait()

    exchange(0, xs, xr)
    cs[...] = cot_ref[...].reshape(SEQ, 4, INNER)
    exchange(1, cs, cr)

    r_i = lax.broadcasted_iota(jnp.int32, (256, 256), 0)
    c_i = lax.broadcasted_iota(jnp.int32, (256, 256), 1)
    to_patch = (c_i == r_i % SEQ * 4 + r_i // SEQ).astype(BF16)
    to_frame = (r_i == c_i % SEQ * 4 + c_i // SEQ).astype(BF16)

    ends = [len_ref[0, 0]]
    for i in range(1, 4):
        ends.append(ends[-1] + len_ref[0, i])
    rows2 = lax.broadcasted_iota(jnp.int32, (128, 128), 0)
    cols2 = lax.broadcasted_iota(jnp.int32, (128, 128), 1)

    def clip_of(frame):
        total = jnp.zeros_like(frame)
        for e in ends:
            total = total + (frame >= e).astype(jnp.int32)
        return total

    same = (rows2 // SEQ == cols2 // SEQ) & (clip_of(rows2 % SEQ) == clip_of(cols2 % SEQ))
    amask[...] = jnp.where(same, 0.0, -jnp.inf).astype(F32)

    arrived(0, xs, xr)
    xp = dot(to_patch, xr[...].reshape(256, INNER)).astype(BF16)
    w_in.wait()

    @pl.loop(0, 9)
    def _(n):
        cols = pl.ds(pl.multiple_of(n * 384, 128), 384)
        qkv[:, cols] = dot(xp, inw[:, cols]).astype(BF16)

    @pl.loop(0, 2)
    def _(i):
        rows = pl.ds(pl.multiple_of(i * 128, 128), 128)
        place = Columns(att, rows, 0)
        for h in range(HEADS):
            lo, hi = window(h)
            q = qkv[rows, lo:hi] * lane_mask(h, lo, hi, BF16)
            k = qkv[rows, INNER + lo : INNER + hi]
            v = qkv[rows, 2 * INNER + lo : 2 * INNER + hi]
            s = dot(q, k, NT) * SCALE + amask[...]
            e = jnp.exp(s - jnp.max(s, axis=-1, keepdims=True))
            w = e / jnp.sum(e, axis=-1, keepdims=True)
            w32s[i, h] = w
            place.add(h, dot(w.astype(BF16), v), lo, hi)

    w_out.wait()
    att_f = dot(to_frame, att[...]).astype(BF16)
    ms[...] = dot(att_f, outw[...]).astype(BF16).reshape(SEQ, 4, INNER)
    exchange(2, ms, mixed_o)

    arrived(1, cs, cr)
    cp[...] = dot(to_patch, cr[...].reshape(256, INNER)).astype(BF16)
    attT[...] = att[...].T

    mate = z * 8 + y * 2 + (c + 1) % CS
    mine = pl.ds(pl.multiple_of(c * 576, 16), 576)
    theirs = pl.ds(pl.multiple_of((1 - c) * 576, 16), 576)
    to_mate = [
        pltpu.make_async_remote_copy(
            src_ref=s, dst_ref=d, send_sem=psem_s.at[k], recv_sem=psem_r.at[k],
            device_id=(x, mate), device_id_type=MESH,
        )
        for k, (s, d) in enumerate(((attT.at[theirs], paT), (cp, pc)))
    ]
    for t in to_mate:
        t.start()

    ga[...] = dot(cp[...], outw[...], NT).astype(BF16)

    for t in to_mate:
        t.wait()

    def block(j):
        own = attT[pl.ds(pl.multiple_of(c * 576 + j * 144, 16), 144), :]
        other = paT[pl.ds(pl.multiple_of(j * 144, 16), 144), :]
        return dot(own, cp[...]) + dot(other, pc[...])

    def x_copy(k):
        return pltpu.make_async_remote_copy(
            src_ref=gsend.at[k], dst_ref=gxr.at[k], send_sem=xsem_s.at[k], recv_sem=xsem_r.at[k],
            device_id=((x + k + 1) % XS, me), device_id_type=MESH,
        )

    for k in range(XS - 1):
        gsend[k] = block((x + k + 1) % XS).astype(BF16)
        x_copy(k).start()
    gown[...] = block(x)

    def y_copy(k):
        d = (y + k + 1) % YS
        return pltpu.make_async_remote_copy(
            src_ref=ysend.at[d], dst_ref=yr.at[k], send_sem=ysem_s.at[k], recv_sem=ysem_r.at[k],
            device_id=(x, z * 8 + d * 2 + c), device_id_type=MESH,
        )

    root = 4 * c + x
    z_copy = pltpu.make_async_remote_copy(
        src_ref=zsend, dst_ref=zr.at[z], send_sem=zsem_s, recv_sem=zsem_r,
        device_id=(x, root * 8 + y * 2 + c), device_id_type=MESH,
    )

    def x_stage():
        total = gown[...]
        for k in range(XS - 1):
            x_copy(k).wait()
            total = total + gxr[k].astype(F32)
        gown[...] = total
        for d in range(YS):
            ysend[d] = total[36 * d : 36 * d + 36].astype(BF16)
        for k in range(YS - 1):
            y_copy(k).start()

    def y_stage():
        total = ysend[y].astype(F32)
        for k in range(YS - 1):
            y_copy(k).wait()
            total = total + yr[k].astype(F32)
        zsend[...] = total.astype(BF16)

        @pl.when(z != root)
        def _():
            z_copy.start()

    def b_copy(dx, dc, k):
        return pltpu.make_async_remote_copy(
            src_ref=ogs.at[(c + dc) % CS], dst_ref=ogr, send_sem=bsem_s.at[k], recv_sem=bsem_r,
            device_id=((x + dx) % XS, z * 8 + y * 2 + (c + dc) % CS), device_id_type=MESH,
        )

    others = [(dx, dc) for dx in range(XS) for dc in range(CS) if (dx, dc) != (0, 0)]

    def z_stage():
        @pl.when(z == root)
        def _():
            part = zr.at[pl.ds(0, ZS - 1)]
            pltpu.make_async_copy(part, part, zsem_r).wait()
            zr[z] = zsend[...]
            total = zr[0].astype(F32)
            for k in range(1, ZS):
                total = total + zr[k].astype(F32)
            ogs[0] = total[:18]
            ogs[1] = total[18:]
            for k, (dx, dc) in enumerate(others):
                b_copy(dx, dc, k).start()

        @pl.when(z != root)
        def _():
            z_copy.wait_send()

    def last_stage():
        @pl.when(z == root)
        def _():
            og_o[...] = ogs[c]
            for k, (dx, dc) in enumerate(others):
                b_copy(dx, dc, k).wait_send()

        @pl.when(z != root)
        def _():
            b_copy(1, 0, 0).wait_recv()
            og_o[...] = ogr[...]

    @pl.loop(0, 2)
    def _(i):
        rows = pl.ds(pl.multiple_of(i * 128, 128), 128)
        pq, pk, pv = (Columns(gp, rows, INNER * t) for t in range(3))
        for h in range(HEADS):
            lo, hi = window(h)
            q = qkv[rows, lo:hi]
            k = qkv[rows, INNER + lo : INNER + hi]
            v = qkv[rows, 2 * INNER + lo : 2 * INNER + hi]
            g = ga[rows, lo:hi]
            w = w32s[i, h]
            dw = dot(g * lane_mask(h, lo, hi, BF16), v, NT)
            ds = (w * (dw - jnp.sum(w * dw, axis=-1, keepdims=True)) * SCALE).astype(BF16)
            pv.add(h, dot(w.astype(BF16), g, TN), lo, hi)
            pq.add(h, dot(ds, k), lo, hi)
            pk.add(h, dot(ds, q, TN), lo, hi)

    x_stage()

    @pl.loop(0, 9)
    def _(n):
        cols = pl.ds(pl.multiple_of(n * 128, 128), 128)
        cp[:, cols] = dot(gp[...], inw[cols, :], NT).astype(BF16)

    gs[...] = dot(to_frame, cp[...]).astype(BF16).reshape(SEQ, 4, INNER)
    exchange(3, gs, glat_o)
    y_stage()
    z_stage()
    last_stage()

    sent(0, xs)
    sent(1, cs)
    sent(2, ms)
    sent(3, gs)
    arrived(2, ms, mixed_o)
    arrived(3, gs, glat_o)


def body(latents, in_weight, out_weight, cotangent, clip_lengths):
    width = latents.shape[3]
    vmem = pl.BlockSpec(memory_space=pltpu.VMEM)
    hbm = pl.BlockSpec(memory_space=pl.ANY)
    msg = (SEQ, 4, INNER)
    tok = (256, INNER)
    dma = pltpu.SemaphoreType.DMA
    mixed, grad_latents, out_grad = pl.pallas_call(
        kernel,
        out_shape=[
            jax.ShapeDtypeStruct(msg, BF16),
            jax.ShapeDtypeStruct(msg, BF16),
            jax.ShapeDtypeStruct((18, INNER), F32),
        ],
        in_specs=[vmem, vmem, pl.BlockSpec(memory_space=pltpu.SMEM), hbm, hbm],
        out_specs=[hbm, hbm, vmem],
        scratch_shapes=[pltpu.VMEM(msg, BF16)] * 6
        + [
            pltpu.VMEM((INNER, 3 * INNER), BF16),
            pltpu.VMEM((INNER, INNER), BF16),
            pltpu.VMEM((256, 3 * INNER), BF16),
            pltpu.VMEM((2, HEADS, 128, 128), F32),
            pltpu.VMEM(tok, BF16),
            pltpu.VMEM(tok, BF16),
            pltpu.VMEM(tok, BF16),
            pltpu.VMEM((256, 3 * INNER), BF16),
            pltpu.VMEM((INNER, 256), BF16),
            pltpu.VMEM((576, 256), BF16),
            pltpu.VMEM(tok, BF16),
            pltpu.VMEM((3, 144, INNER), BF16),
            pltpu.VMEM((3, 144, INNER), BF16),
            pltpu.VMEM((144, INNER), F32),
            pltpu.VMEM((4, 36, INNER), BF16),
            pltpu.VMEM((3, 36, INNER), BF16),
            pltpu.VMEM((36, INNER), BF16),
            pltpu.VMEM((ZS, 36, INNER), BF16),
            pltpu.VMEM((2, 18, INNER), F32),
            pltpu.VMEM((18, INNER), F32),
            pltpu.VMEM((128, 128), F32),
            dma((2,)), dma((4,)), dma((4,)), dma((4,)),
            dma((2,)), dma((2,)), dma((3,)), dma((3,)), dma((3,)), dma((3,)),
            dma, dma, dma((7,)), dma,
        ],
        compiler_params=pltpu.CompilerParams(
            collective_id=0, has_side_effects=True, vmem_limit_bytes=56 << 20
        ),
        name="sublayer",
    )(
        latents.reshape(256, width), cotangent.reshape(256, width), clip_lengths, in_weight, out_weight,
    )
    return mixed.reshape(latents.shape), grad_latents.reshape(latents.shape), out_grad


def solution(mesh):
    placed = (P("dp", "seq", None, None), P(), P(), P("dp", "seq", None, None), P("dp", None))
    return jax.shard_map(
        body,
        mesh=mesh,
        in_specs=placed,
        out_specs=(P("dp", "seq", None, None), P("dp", "seq", None, None), P("seq", None)),
        check_vma=False,
    )
```

time: 570 us -> 104 us (0.18)
  the two profiles are of different devices: /device:TPU:128 before, /device:TPU:33 now
where the time goes in v1:
time: 104 us
  Pallas kernels  97 us (93%)
  local copies, waits for them, and re-layouts  5.9 us (6%)
    pallas_call x1, Pallas kernels, body(): pl.pallas_call(kernel, out_shape=[jax.ShapeDtypeStruct(msg, BF16), jax.Sh...  97 us
    reshape x1, local copies, waits for them, and re-layouts, body(): mixed.reshape(latents.shape)  2.18 us
    reshape x1, local copies, waits for them, and re-layouts, body(): grad_latents.reshape(latents.shape)  2.17 us

profile of v1, /device:TPU:33, one launch (start us, length us, event | category | flops | bytes accessed | tf_op | source)
XLA Modules:
  0.0 103.6 jit_solution(16127416981345518885)
XLA Ops:
  0.6 97.0 %sublayer.1 = (bf16[64,4,1152]{2,1,0:T(4,128)(2,1)}, bf16[64,4,1152]{2,1,0:T(4,128)(2,1)}, f32[18,1152]{1,0:T(8,128)}) custom-call(bf16[256,1152]{1,0:T(8,128)(2,1)} %bitcast.2, bf16[256,1152]{1,0:T(8,128)(2,1)} %bitcast.3, s32[1,4]{1,0:T(1,128)} %len_ref.1, bf16[1152,3456]{1,0:T(8,128)(2,1)} %inw_hbm.1, bf16[1152,1152]{1,0:T(8,128)(2,1)} %outw_hbm.1), custom_call_target="tpu_custom_call" | custom-call | tf_op jit(solution)/shard_map/sublayer/pallas_call | solution.py:319
  97.7 2.2 %reshape.20 = bf16[1,1,256,1152]{3,2,1,0:T(8,128)(2,1)} reshape(bf16[64,4,1152]{2,1,0:T(4,128)(2,1)} %get-tuple-element.6) | data formatting | bytes 1179648 | tf_op jit(solution)/shard_map/reshape | solution.py:362
  99.8 2.2 %reshape.21 = bf16[1,1,256,1152]{3,2,1,0:T(8,128)(2,1)} reshape(bf16[64,4,1152]{2,1,0:T(4,128)(2,1)} %get-tuple-element.7) | data formatting | bytes 1179648 | tf_op jit(solution)/shard_map/reshape | solution.py:362
  102.0 1.5 %copy.9 = f32[18,1152]{1,0:T(8,128)} copy(f32[18,1152]{1,0:T(8,128)} %get-tuple-element.14) | data formatting | bytes 165888

commit v2 on v0

v2 whole, which is shorter than its diff:
```python
import jax
import jax.numpy as jnp
from jax import lax
from jax.experimental import pallas as pl
from jax.experimental.pallas import tpu as pltpu
from jax.sharding import PartitionSpec as P

MESH = pl.DeviceIdType.MESH
BF16 = jnp.bfloat16
F32 = jnp.float32
HEADS, HD = 16, 72
INNER = HEADS * HD
ZS, YS, CS, XS = 8, 4, 2, 4
SEQ = ZS * YS * CS
SCALE = float(HD) ** -0.5
LOG2E = 1.4426950408889634
LEFT = 640
RIGHT = INNER - LEFT
NT = (((1,), (1,)), ((), ()))
NN = (((1,), (0,)), ((), ()))
TN = (((0,), (0,)), ((), ()))
OTHERS = [(dx, dc) for dx in range(XS) for dc in range(CS) if (dx, dc) != (0, 0)]
GROUP = 4


def dot(a, b, dims=NN):
    return lax.dot_general(a, b, dims, preferred_element_type=F32)


def kernel(
    lat_hbm, cot_hbm, len_ref, inw_hbm, outw_hbm,
    mixed_o, glat_o, og_o,
    latv, cotv, xs, xr, cs, cr, ms, gs, inw, inwT, outw, qkvT, w32s, attT, cp, gaT, gpT, glatT, paT, pc,
    gsx, grx, gsy, gry, gox, goy, ys1, yr1, ys2, yr2, zs1, zr1, zs2, zr2, og1s, og2s, og1, og2, amask,
    wsem, lsem, ssem, rsem, psem_s, psem_r, gsem_s, gsem_r, hsem_s, hsem_r, zsem_s, zsem_r, bsem_s, bsem_r,
):
    x = lax.axis_index("dp")
    me = lax.axis_index("seq")
    z, y, c = me // (YS * CS), me // CS % YS, me % CS

    def seq(zz, yy, cc):
        return zz * (YS * CS) + yy * CS + cc

    loads = [
        pltpu.make_async_copy(s, d, wsem.at[k])
        for k, (s, d) in enumerate(((lat_hbm, latv), (cot_hbm, cotv), (inw_hbm, inw), (outw_hbm, outw)))
    ]
    for t in loads:
        t.start()

    def peer(j):
        i, r = j // 8, 7 - j % 8
        dz = 4 + i // 2 - i % 2 * i
        return seq((z + dz) % ZS, (y + r // CS) % YS, (c + r) % CS)

    barrier = pltpu.get_barrier_semaphore()

    @pl.loop(0, SEQ - 1, unroll=9)
    def _(j):
        pl.semaphore_signal(barrier, inc=1, device_id=(x, peer(j)), device_id_type=MESH)

    for dx, dc in OTHERS[1:]:
        pl.semaphore_signal(
            barrier, inc=1, device_id=((x + dx) % XS, seq(z, y, (c + dc) % CS)), device_id_type=MESH
        )

    loads[0].wait()
    xs[...] = latv[...].reshape(SEQ, 4, INNER)
    pl.semaphore_wait(barrier, SEQ - 1 + len(OTHERS) - 1)

    def exchange(k, src, dst):
        @pl.loop(0, SEQ - 1, unroll=9)
        def _(j):
            d = peer(j)
            pltpu.make_async_remote_copy(
                src_ref=src.at[d], dst_ref=dst.at[me], send_sem=ssem.at[k], recv_sem=rsem.at[k],
                device_id=(x, d), device_id_type=MESH,
            ).start()

        pltpu.make_async_copy(src.at[me], dst.at[me], lsem.at[k]).start()

    def arrived(k, src, dst):
        pltpu.make_async_copy(src.at[me], dst.at[me], lsem.at[k]).wait()
        part = dst.at[pl.ds(0, SEQ - 1)]
        pltpu.make_async_copy(part, part, rsem.at[k]).wait()

    def sent(k, src):
        part = src.at[pl.ds(0, SEQ - 1)]
        pltpu.make_async_copy(part, part, ssem.at[k]).wait()

    exchange(0, xs, xr)
    loads[1].wait()
    cs[...] = cotv[...].reshape(SEQ, 4, INNER)

    r_i = lax.broadcasted_iota(jnp.int32, (256, 256), 0)
    c_i = lax.broadcasted_iota(jnp.int32, (256, 256), 1)
    to_patch = (c_i == r_i % SEQ * 4 + r_i // SEQ).astype(BF16)
    to_frame = (r_i == c_i % SEQ * 4 + c_i // SEQ).astype(BF16)

    ends = [len_ref[0, 0]]
    for i in range(1, 4):
        ends.append(ends[-1] + len_ref[0, i])
    rows2 = lax.broadcasted_iota(jnp.int32, (128, 128), 0)
    cols2 = lax.broadcasted_iota(jnp.int32, (128, 128), 1)

    def clip_of(frame):
        total = jnp.zeros_like(frame)
        for e in ends:
            total = total + (frame >= e).astype(jnp.int32)
        return total

    same = (rows2 // SEQ == cols2 // SEQ) & (clip_of(rows2 % SEQ) == clip_of(cols2 % SEQ))
    amask[...] = jnp.where(same, 0.0, -jnp.inf).astype(F32)

    loads[2].wait()

    @pl.loop(0, 9)
    def _(n):
        cols = pl.ds(pl.multiple_of(n * 384, 128), 384)
        inwT[cols, :] = inw[:, cols].T

    exchange(1, cs, cr)
    loads[3].wait()

    arrived(0, xs, xr)
    xp = dot(to_patch, xr[...].reshape(256, INNER)).astype(BF16)

    @pl.loop(0, 6)
    def _(n):
        out = dot(inwT[pl.ds(pl.multiple_of(n * 576, 16), 576), :], xp, NT)
        for i in range(8):
            qkvT[n * 8 + i] = out[HD * i : HD * i + HD].astype(BF16)


    def lanes(i):
        return slice(128 * i, 128 * i + 128)

    @pl.loop(0, HEADS // GROUP)
    def _(n):
        for i in range(2):
            outs = []
            for t in range(GROUP):
                h = n * GROUP + t
                s = dot(qkvT[HEADS + h, :, lanes(i)], qkvT[h, :, lanes(i)], TN) + amask[...]
                e = jnp.exp2((s - jnp.max(s, axis=0, keepdims=True)) * (SCALE * LOG2E))
                w = e / jnp.sum(e, axis=0, keepdims=True)
                w32s[i, h] = w
                outs.append(dot(qkvT[2 * HEADS + h, :, lanes(i)], w.astype(BF16)))
            rows = pl.ds(pl.multiple_of(n * (GROUP * HD), 16), GROUP * HD)
            attT[rows, lanes(i)] = jnp.concatenate(outs, axis=0).astype(BF16)

    mate = seq(z, y, 1 - c)
    theirs = pl.ds(pl.multiple_of((1 - c) * 576, 16), 576)

    def to_mate(k, src, dst):
        return pltpu.make_async_remote_copy(
            src_ref=src, dst_ref=dst, send_sem=psem_s.at[k], recv_sem=psem_r.at[k],
            device_id=(x, mate), device_id_type=MESH,
        )

    att_copy = to_mate(0, attT.at[theirs], paT)
    cot_copy = to_mate(1, cp, pc)
    att_copy.start()
    att_f = dot(to_frame, attT[...], NT).astype(BF16)
    ms[...] = dot(att_f, outw[...]).astype(BF16).reshape(SEQ, 4, INNER)
    exchange(2, ms, mixed_o)

    arrived(1, cs, cr)
    cp[...] = dot(to_patch, cr[...].reshape(256, INNER)).astype(BF16)
    cot_copy.start()

    @pl.loop(0, 2)
    def _(n):
        out = dot(outw[pl.ds(pl.multiple_of(n * 576, 16), 576), :], cp[...], NT)
        for i in range(8):
            gaT[n * 8 + i] = out[HD * i : HD * i + HD].astype(BF16)

    att_copy.wait()
    cot_copy.wait()

    def block(j, cols):
        own = attT[pl.ds(pl.multiple_of(c * 576 + j * 144, 16), 144), :]
        other = paT[pl.ds(pl.multiple_of(j * 144, 16), 144), :]
        return dot(own, cp[:, cols]) + dot(other, pc[:, cols])

    left, right = slice(0, LEFT), slice(LEFT, INNER)

    def x_copy(k, src, dst, s, r):
        return pltpu.make_async_remote_copy(
            src_ref=src, dst_ref=dst.at[k], send_sem=s.at[k], recv_sem=r.at[k],
            device_id=((x + k + 1) % XS, me), device_id_type=MESH,
        )

    def y_copy(k, src, dst, s, r):
        return pltpu.make_async_remote_copy(
            src_ref=src, dst_ref=dst.at[k], send_sem=s.at[k], recv_sem=r.at[k],
            device_id=(x, seq(z, (y + k + 1) % YS, c)), device_id_type=MESH,
        )

    def first(k, p):
        if p == 0:
            return x_copy(k, gsx.at[k], grx, gsem_s.at[0], gsem_r.at[0])
        return y_copy(k, gsy.at[k], gry, gsem_s.at[1], gsem_r.at[1])

    def second(k, p):
        if p == 0:
            return y_copy(k, ys1.at[(y + k + 1) % YS], yr1, hsem_s.at[0], hsem_r.at[0])
        return x_copy(k, ys2.at[(x + k + 1) % XS], yr2, hsem_s.at[1], hsem_r.at[1])

    for k in range(3):
        gsx[k] = block((x + k + 1) % XS, left).astype(BF16)
        first(k, 0).start()
        gsy[k] = block((y + k + 1) % YS, right).astype(BF16)
        first(k, 1).start()
    gox[...] = block(x, left)
    goy[...] = block(y, right)

    def first_sum():
        for p, (own, got, out) in enumerate(((gox, grx, ys1), (goy, gry, ys2))):
            total = own[...]
            for k in range(3):
                first(k, p).wait()
                total = total + got[k].astype(F32)
            for d in range(4):
                out[d] = total[36 * d : 36 * d + 36].astype(BF16)
            for k in range(3):
                second(k, p).start()

    root1, root2 = seq(4 * c + x, y, c), seq(4 * c + y, x, c)
    z_copies = [
        pltpu.make_async_remote_copy(
            src_ref=src, dst_ref=dst.at[z], send_sem=zsem_s.at[p], recv_sem=zsem_r.at[p],
            device_id=(x, root), device_id_type=MESH,
        )
        for p, (src, dst, root) in enumerate(((zs1, zr1, root1), (zs2, zr2, root2)))
    ]
    is_root = (z == 4 * c + x, (y == x) & (z // 4 == c))

    def second_sum():
        for p, (mine, got, src, at, root, dst) in enumerate(
            ((ys1, yr1, zs1, y, root1, zr1), (ys2, yr2, zs2, x, root2, zr2))
        ):
            total = mine[at].astype(F32)
            for k in range(3):
                second(k, p).wait()
                total = total + got[k].astype(F32)
            src[...] = total.astype(BF16)

            @pl.when(root != me)
            def _():
                z_copies[p].start()

            @pl.when(root == me)
            def _():
                dst[z] = src[...]

    def b_copy(p, k, src, dst):
        dx, dc = OTHERS[k]
        return pltpu.make_async_remote_copy(
            src_ref=src.at[(c + dc) % CS], dst_ref=dst, send_sem=bsem_s.at[p, k], recv_sem=bsem_r.at[p],
            device_id=((x + dx) % XS, seq(z, y, (c + dc) % CS)), device_id_type=MESH,
        )

    parts = ((zr1, og1s, og1, root1), (zr2, og2s, og2, root2))

    def z_sum():
        for p, (got, out, dst, root) in enumerate(parts):

            @pl.when(is_root[p])
            def _():
                few, all_ = got.at[pl.ds(0, ZS - 1)], got

                @pl.when(root == me)
                def _():
                    pltpu.make_async_copy(few, few, zsem_r.at[p]).wait()

                @pl.when(root != me)
                def _():
                    pltpu.make_async_copy(all_, all_, zsem_r.at[p]).wait()

                total = got[0].astype(F32)
                for k in range(1, ZS):
                    total = total + got[k].astype(F32)
                out[0] = total[:18]
                out[1] = total[18:]
                for k in range(len(OTHERS)):
                    b_copy(p, k, out, dst).start()

    def last():
        for p, (got, out, dst, root) in enumerate(parts):
            cols = (left, right)[p]

            @pl.when(root != me)
            def _():
                z_copies[p].wait_send()

            @pl.when(is_root[p])
            def _():
                og_o[:, cols] = out[c]
                for k in range(len(OTHERS)):
                    b_copy(p, k, out, dst).wait_send()

            @pl.when(jnp.logical_not(is_root[p]))
            def _():
                b_copy(p, 0, out, dst).wait_recv()
                og_o[:, cols] = dst[...]


    @pl.loop(0, HEADS // GROUP)
    def _(n):
        rows = [
            pl.ds(pl.multiple_of(INNER * t + n * (GROUP * HD), 16), GROUP * HD) for t in range(3)
        ]
        for i in range(2):
            outs = ([], [], [])
            for t in range(GROUP):
                h = n * GROUP + t
                q, k, v = (qkvT[HEADS * u + h, :, lanes(i)] for u in range(3))
                g = gaT[h, :, lanes(i)]
                w = w32s[i, h]
                dw = dot(v, g, TN)
                ds = (w * (dw - jnp.sum(w * dw, axis=0, keepdims=True)) * SCALE).astype(BF16)
                outs[0].append(dot(k, ds))
                outs[1].append(dot(q, ds, NT))
                outs[2].append(dot(g, w.astype(BF16), NT))
            for u in range(3):
                gpT[rows[u], lanes(i)] = jnp.concatenate(outs[u], axis=0).astype(BF16)

    first_sum()

    @pl.loop(0, 2)
    def _(n):
        rows = pl.ds(pl.multiple_of(n * 576, 16), 576)
        glatT[rows, :] = dot(inw[rows, :], gpT[...]).astype(BF16)

    gs[...] = dot(to_frame, glatT[...], NT).astype(BF16).reshape(SEQ, 4, INNER)
    second_sum()
    exchange(3, gs, glat_o)
    z_sum()
    last()
    sent(0, xs)
    sent(1, cs)
    sent(2, ms)
    sent(3, gs)
    arrived(2, ms, mixed_o)
    arrived(3, gs, glat_o)


def unpack(mixed, glat, og, mixed_o, glat_o, og_o):
    mixed_o[0, 0] = mixed[...].reshape(256, INNER)
    glat_o[0, 0] = glat[...].reshape(256, INNER)
    og_o[...] = og[...]


def body(latents, in_weight, out_weight, cotangent, clip_lengths):
    width = latents.shape[3]
    vmem = pl.BlockSpec(memory_space=pltpu.VMEM)
    hbm = pl.BlockSpec(memory_space=pl.ANY)
    msg = (SEQ, 4, INNER)
    tok = (256, INNER)
    dma = pltpu.SemaphoreType.DMA
    mixed, grad_latents, out_grad = pl.pallas_call(
        kernel,
        out_shape=[
            jax.ShapeDtypeStruct(msg, BF16),
            jax.ShapeDtypeStruct(msg, BF16),
            jax.ShapeDtypeStruct((18, INNER), F32),
        ],
        in_specs=[hbm, hbm, pl.BlockSpec(memory_space=pltpu.SMEM), hbm, hbm],
        out_specs=[hbm, hbm, vmem],
        scratch_shapes=[pltpu.VMEM(tok, BF16)] * 2
        + [pltpu.VMEM(msg, BF16)] * 6
        + [
            pltpu.VMEM((INNER, 3 * INNER), BF16),
            pltpu.VMEM((3 * INNER, INNER), BF16),
            pltpu.VMEM((INNER, INNER), BF16),
            pltpu.VMEM((3 * HEADS, HD, 256), BF16),
            pltpu.VMEM((2, HEADS, 128, 128), F32),
            pltpu.VMEM((INNER, 256), BF16),
            pltpu.VMEM(tok, BF16),
            pltpu.VMEM((HEADS, HD, 256), BF16),
            pltpu.VMEM((3 * INNER, 256), BF16),
            pltpu.VMEM((INNER, 256), BF16),
            pltpu.VMEM((576, 256), BF16),
            pltpu.VMEM(tok, BF16),
            pltpu.VMEM((3, 144, LEFT), BF16),
            pltpu.VMEM((3, 144, LEFT), BF16),
            pltpu.VMEM((3, 144, RIGHT), BF16),
            pltpu.VMEM((3, 144, RIGHT), BF16),
            pltpu.VMEM((144, LEFT), F32),
            pltpu.VMEM((144, RIGHT), F32),
            pltpu.VMEM((4, 36, LEFT), BF16),
            pltpu.VMEM((3, 36, LEFT), BF16),
            pltpu.VMEM((4, 36, RIGHT), BF16),
            pltpu.VMEM((3, 36, RIGHT), BF16),
            pltpu.VMEM((36, LEFT), BF16),
            pltpu.VMEM((ZS, 36, LEFT), BF16),
            pltpu.VMEM((36, RIGHT), BF16),
            pltpu.VMEM((ZS, 36, RIGHT), BF16),
            pltpu.VMEM((2, 18, LEFT), F32),
            pltpu.VMEM((2, 18, RIGHT), F32),
            pltpu.VMEM((18, LEFT), F32),
            pltpu.VMEM((18, RIGHT), F32),
            pltpu.VMEM((128, 128), F32),
            dma((4,)), dma((4,)), dma((4,)), dma((4,)), dma((2,)), dma((2,)),
            dma((2, 3)), dma((2, 3)), dma((2, 3)), dma((2, 3)), dma((2,)), dma((2,)),
            dma((2, 7)), dma((2,)),
        ],
        compiler_params=pltpu.CompilerParams(
            collective_id=0, has_side_effects=True, vmem_limit_bytes=52 << 20
        ),
        name="sublayer",
    )(
        latents.reshape(256, width), cotangent.reshape(256, width), clip_lengths, in_weight, out_weight,
    )
    return pl.pallas_call(
        unpack,
        out_shape=[
            jax.ShapeDtypeStruct(latents.shape, BF16),
            jax.ShapeDtypeStruct(latents.shape, BF16),
            jax.ShapeDtypeStruct((18, INNER), F32),
        ],
        in_specs=[vmem] * 3,
        out_specs=[vmem] * 3,
        compiler_params=pltpu.CompilerParams(vmem_limit_bytes=8 << 20),
        name="unpack",
    )(mixed, grad_latents, out_grad)


def solution(mesh):
    placed = (P("dp", "seq", None, None), P(), P(), P("dp", "seq", None, None), P("dp", None))
    return jax.shard_map(
        body,
        mesh=mesh,
        in_specs=placed,
        out_specs=(P("dp", "seq", None, None), P("dp", "seq", None, None), P("seq", None)),
        check_vma=False,
    )
```

time: 570 us -> 83.9 us (0.15)
  the two profiles are of different devices: /device:TPU:128 before, /device:TPU:1 now
where the time goes in v2:
time: 83.9 us; the launch traced here: 83.7 us
  Pallas kernels  81.4 us (97%)
  local copies, waits for them, and re-layouts  1.71 us (2%)
    pallas_call x1, Pallas kernels, body(): pl.pallas_call(kernel, out_shape=[jax.ShapeDtypeStruct(msg, BF16), jax.Sh...  80.2 us
    unnamed x4, local copies, waits for them, and re-layouts  1.71 us

profile of v2, /device:TPU:1, one launch (start us, length us, event | category | flops | bytes accessed | tf_op | source)
XLA Modules:
  0.0 83.7 jit_solution(11073948655137558383)
XLA Ops:
  0.6 0.0 copy-start
  0.6 1.1 %copy-done = bf16[1,1,256,1152]{3,2,1,0:T(8,128)(2,1)S(1)} copy-done((bf16[1,1,256,1152]{3,2,1,0:T(8,128)(2,1)S(1)}, bf16[1,1,256,1152]{3,2,1,0:T(8,128)(2,1)}, u32[]{:S(2)}) %copy-start) | copy-done | bytes 589848
  1.7 0.0 copy-start.1
  1.7 0.7 copy-done.1
  2.4 80.2 %sublayer.1 = (bf16[64,4,1152]{2,1,0:T(4,128)(2,1)S(1)}, bf16[64,4,1152]{2,1,0:T(4,128)(2,1)S(1)}, f32[18,1152]{1,0:T(8,128)S(1)}) custom-call(bf16[256,1152]{1,0:T(8,128)(2,1)S(1)} %bitcast.2, bf16[256,1152]{1,0:T(8,128)(2,1)} %bitcast.3, s32[1,4]{1,0:T(1,128)S(1)} %copy-done.1, bf16[1152,3456]{1,0:T(8,128)(2,1)} %inw_hbm.1, bf16[1152,1152]{1,0:T(8,128)(2,1)} %outw_hbm.1), custom_call_target="tpu_custom_call" | custom-call | tf_op jit(solution)/shard_map/sublayer/pallas_call | solution.py:362
  82.5 1.2 %unpack.1 = (bf16[1,1,256,1152]{3,2,1,0:T(8,128)(2,1)}, bf16[1,1,256,1152]{3,2,1,0:T(8,128)(2,1)}, f32[18,1152]{1,0:T(8,128)}) custom-call(bf16[64,4,1152]{2,1,0:T(4,128)(2,1)S(1)} %get-tuple-element.6.mixed, bf16[64,4,1152]{2,1,0:T(4,128)(2,1)S(1)} %get-tuple-element.7.glat, f32[18,1152]{1,0:T(8,128)S(1)} %get-tuple-element.8.og), custom_call_target="tpu_custom_call" | custom-call | tf_op jit(solution)/shard_map/unpack/pallas_call | solution.py:416
Async XLA Ops:
  0.6 1.1 %copy-start = (bf16[1,1,256,1152]{3,2,1,0:T(8,128)(2,1)S(1)}, bf16[1,1,256,1152]{3,2,1,0:T(8,128)(2,1)}, u32[]{:S(2)}) copy-start(bf16[1,1,256,1152]{3,2,1,0:T(8,128)(2,1)} %param.5) | copy-start | bytes 1769476
  1.7 0.7 copy-start.1

commit v3 on v2

v3 whole, which is shorter than its diff:
```python
import jax
import jax.numpy as jnp
from jax import lax
from jax.experimental import pallas as pl
from jax.experimental.pallas import tpu as pltpu
from jax.sharding import PartitionSpec as P

MESH = pl.DeviceIdType.MESH
BF16 = jnp.bfloat16
F32 = jnp.float32
HEADS, HD = 16, 72
INNER = HEADS * HD
ZS, YS, CS, XS = 8, 4, 2, 4
SEQ = ZS * YS * CS
SCALE = float(HD) ** -0.5
LOG2E = 1.4426950408889634
PARTS = (384, 768, 1152)
COLS = [slice(a, b) for a, b in zip((0,) + PARTS, PARTS)]
WIDTHS = [c.stop - c.start for c in COLS]
NP = len(PARTS)
NT = (((1,), (1,)), ((), ()))
NN = (((1,), (0,)), ((), ()))
TN = (((0,), (0,)), ((), ()))
OTHERS = [(dx, dc) for dx in range(XS) for dc in range(CS) if (dx, dc) != (0, 0)]
GROUP = 4
BATCH = 9


def dot(a, b, dims=NN):
    return lax.dot_general(a, b, dims, preferred_element_type=F32)


def kernel(*refs):
    lat_hbm, cot_hbm, len_ref, inw_hbm, outw_hbm, mixed_o, glat_o, og_o = refs[:8]
    (
        latv, cotv, xs, xr, ms, gs, inw, inwT, outw, qkvT, w32s, attT, cp, gaT, gpT, glatT, paT, pc,
        zs, zr, ogs, ogr, amask,
    ) = refs[8:31]
    (
        wsem, lsem, ssem, rsem, psem_s, psem_r, gsem_s, gsem_r, hsem_s, hsem_r,
        zsem_s, zsem_r, bsem_s, bsem_r,
    ) = refs[31:45]
    csp, crp, gsp, grp, gop, hsp, hrp = (refs[45 + NP * i : 45 + NP * i + NP] for i in range(7))
    x = lax.axis_index("dp")
    me = lax.axis_index("seq")
    z, y, c = me // (YS * CS), me // CS % YS, me % CS

    def seq(zz, yy, cc):
        return zz * (YS * CS) + yy * CS + cc

    loads = [
        pltpu.make_async_copy(s, d, wsem.at[k])
        for k, (s, d) in enumerate(((lat_hbm, latv), (cot_hbm, cotv), (inw_hbm, inw), (outw_hbm, outw)))
    ]
    for t in loads:
        t.start()

    def peer(i, r):
        dz = 4 + i // 2 - i % 2 * i
        return seq((z + dz) % ZS, (y + r // CS) % YS, (c + r) % CS)

    barrier = pltpu.get_barrier_semaphore()

    @pl.loop(0, SEQ - 1, unroll=9)
    def _(j):
        pl.semaphore_signal(barrier, inc=1, device_id=(x, peer(j // 8, 7 - j % 8)), device_id_type=MESH)

    for dx, dc in OTHERS[1:]:
        pl.semaphore_signal(
            barrier, inc=1, device_id=((x + dx) % XS, seq(z, y, (c + dc) % CS)), device_id_type=MESH
        )

    loads[0].wait()
    xs[...] = latv[...].reshape(SEQ, 4, INNER)
    pl.semaphore_wait(barrier, SEQ - 1 + len(OTHERS) - 1)

    def batch(k, src, dst, b, size=BATCH, sem=0):
        @pl.loop(0, size, unroll=9)
        def _(j):
            n = b * BATCH + j
            d = peer(n % 8, 7 - n // 8)
            pltpu.make_async_remote_copy(
                src_ref=src.at[d], dst_ref=dst.at[me], send_sem=ssem.at[k, sem], recv_sem=rsem.at[k],
                device_id=(x, d), device_id_type=MESH,
            ).start()

    def keep(k, src, dst):
        return pltpu.make_async_copy(src.at[me], dst.at[me], lsem.at[k])

    def exchange(k, src, dst):
        batch(k, src, dst, 0, SEQ - 1)
        keep(k, src, dst).start()

    def arrived(k, src, dst):
        keep(k, src, dst).wait()
        part = dst.at[pl.ds(0, SEQ - 1)]
        pltpu.make_async_copy(part, part, rsem.at[k]).wait()

    def sent(k, src, sem=0, size=SEQ - 1):
        part = src.at[pl.ds(0, size)]
        pltpu.make_async_copy(part, part, ssem.at[k, sem]).wait()

    exchange(0, xs, xr)
    loads[1].wait()
    for p in range(NP):
        csp[p][...] = cotv[:, COLS[p]].reshape(SEQ, 4, WIDTHS[p])

    r_i = lax.broadcasted_iota(jnp.int32, (256, 256), 0)
    c_i = lax.broadcasted_iota(jnp.int32, (256, 256), 1)
    to_patch = (c_i == r_i % SEQ * 4 + r_i // SEQ).astype(BF16)
    to_frame = (r_i == c_i % SEQ * 4 + c_i // SEQ).astype(BF16)

    ends = [len_ref[0, 0]]
    for i in range(1, 4):
        ends.append(ends[-1] + len_ref[0, i])
    rows2 = lax.broadcasted_iota(jnp.int32, (128, 128), 0)
    cols2 = lax.broadcasted_iota(jnp.int32, (128, 128), 1)

    def clip_of(frame):
        total = jnp.zeros_like(frame)
        for e in ends:
            total = total + (frame >= e).astype(jnp.int32)
        return total

    same = (rows2 // SEQ == cols2 // SEQ) & (clip_of(rows2 % SEQ) == clip_of(cols2 % SEQ))
    amask[...] = jnp.where(same, 0.0, -jnp.inf).astype(F32)

    loads[2].wait()

    @pl.loop(0, 9)
    def _(n):
        cols = pl.ds(pl.multiple_of(n * 384, 128), 384)
        inwT[cols, :] = inw[:, cols].T

    for p in range(NP):
        exchange(3 + p, csp[p], crp[p])
    loads[3].wait()

    arrived(0, xs, xr)
    xp = dot(to_patch, xr[...].reshape(256, INNER)).astype(BF16)

    @pl.loop(0, 6)
    def _(n):
        out = dot(inwT[pl.ds(pl.multiple_of(n * 576, 16), 576), :], xp, NT)
        for i in range(8):
            qkvT[n * 8 + i] = out[HD * i : HD * i + HD].astype(BF16)


    def lanes(i):
        return slice(128 * i, 128 * i + 128)

    @pl.loop(0, HEADS // GROUP)
    def _(n):
        for i in range(2):
            outs = []
            for t in range(GROUP):
                h = n * GROUP + t
                s = dot(qkvT[HEADS + h, :, lanes(i)], qkvT[h, :, lanes(i)], TN) + amask[...]
                e = jnp.exp2((s - jnp.max(s, axis=0, keepdims=True)) * (SCALE * LOG2E))
                w = e / jnp.sum(e, axis=0, keepdims=True)
                w32s[i, h] = w
                outs.append(dot(qkvT[2 * HEADS + h, :, lanes(i)], w.astype(BF16)))
            rows = pl.ds(pl.multiple_of(n * (GROUP * HD), 16), GROUP * HD)
            attT[rows, lanes(i)] = jnp.concatenate(outs, axis=0).astype(BF16)

    mate = seq(z, y, 1 - c)
    theirs = pl.ds(pl.multiple_of((1 - c) * 576, 16), 576)

    def to_mate(k, src, dst):
        return pltpu.make_async_remote_copy(
            src_ref=src, dst_ref=dst, send_sem=psem_s.at[k], recv_sem=psem_r.at[k],
            device_id=(x, mate), device_id_type=MESH,
        )

    att_copy = to_mate(0, attT.at[theirs], paT)
    cot_copies = [to_mate(1 + p, cp.at[:, COLS[p]], pc.at[:, COLS[p]]) for p in range(NP)]
    att_copy.start()

    def block(j, cols):
        own = attT[pl.ds(pl.multiple_of(c * 576 + j * 144, 16), 144), :]
        other = paT[pl.ds(pl.multiple_of(j * 144, 16), 144), :]
        return dot(own, cp[:, cols]) + dot(other, pc[:, cols])

    def x_copy(k, src, dst, s, r):
        return pltpu.make_async_remote_copy(
            src_ref=src, dst_ref=dst.at[k], send_sem=s.at[k], recv_sem=r.at[k],
            device_id=((x + k + 1) % XS, me), device_id_type=MESH,
        )

    def y_copy(k, src, dst, s, r):
        return pltpu.make_async_remote_copy(
            src_ref=src, dst_ref=dst.at[k], send_sem=s.at[k], recv_sem=r.at[k],
            device_id=(x, seq(z, (y + k + 1) % YS, c)), device_id_type=MESH,
        )

    def first(k, p):
        return x_copy(k, gsp[p].at[k], grp[p], gsem_s.at[p], gsem_r.at[p])

    def second(k, p):
        return y_copy(k, hsp[p].at[(y + k + 1) % YS], hrp[p], hsem_s.at[p], hsem_r.at[p])

    def cot_part(p):
        arrived(3 + p, csp[p], crp[p])
        cp[:, COLS[p]] = dot(to_patch, crp[p][...].reshape(256, WIDTHS[p])).astype(BF16)
        cot_copies[p].start()

    def blocks(p):
        cot_copies[p].wait()
        for k in range(3):
            gsp[p][k] = block((x + k + 1) % XS, COLS[p]).astype(BF16)
            first(k, p).start()
        gop[p][...] = block(x, COLS[p])

    cot_part(0)
    att_f = dot(to_frame, attT[...], NT).astype(BF16)
    ms[...] = dot(att_f, outw[...]).astype(BF16).reshape(SEQ, 4, INNER)
    att_copy.wait()
    keep(1, ms, mixed_o).start()
    blocks(0)
    cot_part(1)
    batch(1, ms, mixed_o, 0)
    blocks(1)
    cot_part(2)
    batch(1, ms, mixed_o, 1)

    @pl.loop(0, 2)
    def _(n):
        out = dot(outw[pl.ds(pl.multiple_of(n * 576, 16), 576), :], cp[...], NT)
        for i in range(8):
            gaT[n * 8 + i] = out[HD * i : HD * i + HD].astype(BF16)

    blocks(2)
    batch(1, ms, mixed_o, 2)

    def first_sum(p):
        total = gop[p][...]
        for k in range(3):
            first(k, p).wait()
            total = total + grp[p][k].astype(F32)
        for d in range(4):
            hsp[p][d] = total[36 * d : 36 * d + 36].astype(BF16)
        for k in range(3):
            second(k, p).start()

    root = seq(4 * c + x, y, c)
    z_copy = pltpu.make_async_remote_copy(
        src_ref=zs, dst_ref=zr.at[z], send_sem=zsem_s, recv_sem=zsem_r,
        device_id=(x, root), device_id_type=MESH,
    )

    def second_sum():
        for p in range(NP):
            total = hsp[p][y].astype(F32)
            for k in range(3):
                second(k, p).wait()
                total = total + hrp[p][k].astype(F32)
            zs[:, COLS[p]] = total.astype(BF16)

        @pl.when(root != me)
        def _():
            z_copy.start()

        @pl.when(root == me)
        def _():
            zr[z] = zs[...]

    def b_copy(k):
        dx, dc = OTHERS[k]
        return pltpu.make_async_remote_copy(
            src_ref=ogs.at[(c + dc) % CS], dst_ref=ogr, send_sem=bsem_s.at[k], recv_sem=bsem_r,
            device_id=((x + dx) % XS, seq(z, y, (c + dc) % CS)), device_id_type=MESH,
        )

    def z_sum():
        @pl.when(root == me)
        def _():
            part = zr.at[pl.ds(0, ZS - 1)]
            pltpu.make_async_copy(part, part, zsem_r).wait()
            total = zr[0].astype(F32)
            for k in range(1, ZS):
                total = total + zr[k].astype(F32)
            ogs[0] = total[:18].astype(ogs.dtype)
            ogs[1] = total[18:].astype(ogs.dtype)
            for k in range(len(OTHERS)):
                b_copy(k).start()

    def last():
        @pl.when(root == me)
        def _():
            og_o[...] = ogs[c].astype(F32)
            for k in range(len(OTHERS)):
                b_copy(k).wait_send()

        @pl.when(root != me)
        def _():
            z_copy.wait_send()
            b_copy(0).wait_recv()
            og_o[...] = ogr[...].astype(F32)

    def backward(n):
        rows = [
            pl.ds(pl.multiple_of(INNER * t + n * (GROUP * HD), 16), GROUP * HD) for t in range(3)
        ]
        for i in range(2):
            outs = ([], [], [])
            for t in range(GROUP):
                h = n * GROUP + t
                q, k, v = (qkvT[HEADS * u + h, :, lanes(i)] for u in range(3))
                g = gaT[h, :, lanes(i)]
                w = w32s[i, h]
                dw = dot(v, g, TN)
                ds = (w * (dw - jnp.sum(w * dw, axis=0, keepdims=True)) * SCALE).astype(BF16)
                outs[0].append(dot(k, ds))
                outs[1].append(dot(q, ds, NT))
                outs[2].append(dot(g, w.astype(BF16), NT))
            for u in range(3):
                gpT[rows[u], lanes(i)] = jnp.concatenate(outs[u], axis=0).astype(BF16)
        batch(1, ms, mixed_o, n + 3)

    pl.loop(0, HEADS // GROUP)(backward)
    first_sum(0)
    first_sum(1)

    @pl.loop(0, 2)
    def _(n):
        rows = pl.ds(pl.multiple_of(n * 576, 16), 576)
        glatT[rows, :] = dot(inw[rows, :], gpT[...]).astype(BF16)

    first_sum(2)
    gs[...] = dot(to_frame, glatT[...], NT).astype(BF16).reshape(SEQ, 4, INNER)
    batch(2, gs, glat_o, 0, 18)
    second_sum()
    batch(2, gs, glat_o, 18 // BATCH, SEQ - 1 - 18)
    keep(2, gs, glat_o).start()
    z_sum()
    last()
    sent(0, xs)
    for p in range(NP):
        sent(3 + p, csp[p])
    sent(1, ms)
    sent(2, gs)
    arrived(1, ms, mixed_o)
    arrived(2, gs, glat_o)


def unpack(mixed, glat, og, mixed_o, glat_o, og_o):
    mixed_o[0, 0] = mixed[...].reshape(256, INNER)
    glat_o[0, 0] = glat[...].reshape(256, INNER)
    og_o[...] = og[...]


def body(latents, in_weight, out_weight, cotangent, clip_lengths):
    width = latents.shape[3]
    vmem = pl.BlockSpec(memory_space=pltpu.VMEM)
    hbm = pl.BlockSpec(memory_space=pl.ANY)
    msg = (SEQ, 4, INNER)
    tok = (256, INNER)
    dma = pltpu.SemaphoreType.DMA
    mixed, grad_latents, out_grad = pl.pallas_call(
        kernel,
        out_shape=[
            jax.ShapeDtypeStruct(msg, BF16),
            jax.ShapeDtypeStruct(msg, BF16),
            jax.ShapeDtypeStruct((18, INNER), F32),
        ],
        in_specs=[hbm, hbm, pl.BlockSpec(memory_space=pltpu.SMEM), hbm, hbm],
        out_specs=[hbm, hbm, vmem],
        scratch_shapes=[pltpu.VMEM(tok, BF16)] * 2
        + [pltpu.VMEM(msg, BF16)] * 4
        + [
            pltpu.VMEM((INNER, 3 * INNER), BF16),
            pltpu.VMEM((3 * INNER, INNER), BF16),
            pltpu.VMEM((INNER, INNER), BF16),
            pltpu.VMEM((3 * HEADS, HD, 256), BF16),
            pltpu.VMEM((2, HEADS, 128, 128), F32),
            pltpu.VMEM((INNER, 256), BF16),
            pltpu.VMEM(tok, BF16),
            pltpu.VMEM((HEADS, HD, 256), BF16),
            pltpu.VMEM((3 * INNER, 256), BF16),
            pltpu.VMEM((INNER, 256), BF16),
            pltpu.VMEM((576, 256), BF16),
            pltpu.VMEM(tok, BF16),
            pltpu.VMEM((36, INNER), BF16),
            pltpu.VMEM((ZS, 36, INNER), BF16),
            pltpu.VMEM((2, 18, INNER), BF16),
            pltpu.VMEM((18, INNER), BF16),
            pltpu.VMEM((128, 128), F32),
            dma((4,)), dma((3 + NP,)), dma((3 + NP, 1)), dma((3 + NP,)), dma((1 + NP,)), dma((1 + NP,)),
            dma((NP, 3)), dma((NP, 3)), dma((NP, 3)), dma((NP, 3)), dma, dma,
            dma((7,)), dma,
        ]
        + [pltpu.VMEM((SEQ, 4, w), BF16) for w in WIDTHS] * 2
        + [pltpu.VMEM((3, 144, w), BF16) for w in WIDTHS] * 2
        + [pltpu.VMEM((144, w), F32) for w in WIDTHS]
        + [pltpu.VMEM((4, 36, w), BF16) for w in WIDTHS]
        + [pltpu.VMEM((3, 36, w), BF16) for w in WIDTHS],
        compiler_params=pltpu.CompilerParams(
            collective_id=0, has_side_effects=True, vmem_limit_bytes=52 << 20
        ),
        name="sublayer",
    )(
        latents.reshape(256, width), cotangent.reshape(256, width), clip_lengths, in_weight, out_weight,
    )
    return pl.pallas_call(
        unpack,
        out_shape=[
            jax.ShapeDtypeStruct(latents.shape, BF16),
            jax.ShapeDtypeStruct(latents.shape, BF16),
            jax.ShapeDtypeStruct((18, INNER), F32),
        ],
        in_specs=[vmem] * 3,
        out_specs=[vmem] * 3,
        compiler_params=pltpu.CompilerParams(vmem_limit_bytes=8 << 20),
        name="unpack",
    )(mixed, grad_latents, out_grad)


def solution(mesh):
    placed = (P("dp", "seq", None, None), P(), P(), P("dp", "seq", None, None), P("dp", None))
    return jax.shard_map(
        body,
        mesh=mesh,
        in_specs=placed,
        out_specs=(P("dp", "seq", None, None), P("dp", "seq", None, None), P("seq", None)),
        check_vma=False,
    )
```

time: 83.9 us -> 79.4 us (0.946)
  Pallas kernels: 81.4 us -> 76.9 us
    pallas_call x1, Pallas kernels: 80.2 us -> 75.7 us  [body(): pl.pallas_call(kernel, out_shape=[jax.ShapeDtypeStruct(msg, BF16), jax.Sh...]
where the time goes in v3:
time: 79.4 us; the launch traced here: 79.2 us
  Pallas kernels  76.9 us (97%)
  local copies, waits for them, and re-layouts  1.71 us (2%)
    pallas_call x1, Pallas kernels, body(): pl.pallas_call(kernel, out_shape=[jax.ShapeDtypeStruct(msg, BF16), jax.Sh...  75.7 us
    unnamed x4, local copies, waits for them, and re-layouts  1.71 us

profile of v3, /device:TPU:1, one launch (start us, length us, event | category | flops | bytes accessed | tf_op | source)
XLA Modules:
  0.0 79.2 jit_solution(13918580972348191765)
XLA Ops:
  0.6 0.0 copy-start
  0.6 1.1 %copy-done = bf16[1,1,256,1152]{3,2,1,0:T(8,128)(2,1)S(1)} copy-done((bf16[1,1,256,1152]{3,2,1,0:T(8,128)(2,1)S(1)}, bf16[1,1,256,1152]{3,2,1,0:T(8,128)(2,1)}, u32[]{:S(2)}) %copy-start) | copy-done | bytes 589848
  1.7 0.0 copy-start.1
  1.7 0.7 copy-done.1
  2.4 75.7 %sublayer.1 = (bf16[64,4,1152]{2,1,0:T(4,128)(2,1)S(1)}, bf16[64,4,1152]{2,1,0:T(4,128)(2,1)S(1)}, f32[18,1152]{1,0:T(8,128)S(1)}) custom-call(bf16[256,1152]{1,0:T(8,128)(2,1)S(1)} %bitcast.2, bf16[256,1152]{1,0:T(8,128)(2,1)} %bitcast.3, s32[1,4]{1,0:T(1,128)S(1)} %copy-done.1, bf16[1152,3456]{1,0:T(8,128)(2,1)} %refs_3_.1, bf16[1152,1152]{1,0:T(8,128)(2,1)} %refs_4_.1), custom_call_target="tpu_custom_call" | custom-call | tf_op jit(solution)/shard_map/sublayer/pallas_call | solution.py:359
  78.1 1.2 %unpack.1 = (bf16[1,1,256,1152]{3,2,1,0:T(8,128)(2,1)}, bf16[1,1,256,1152]{3,2,1,0:T(8,128)(2,1)}, f32[18,1152]{1,0:T(8,128)}) custom-call(bf16[64,4,1152]{2,1,0:T(4,128)(2,1)S(1)} %get-tuple-element.6.mixed, bf16[64,4,1152]{2,1,0:T(4,128)(2,1)S(1)} %get-tuple-element.7.glat, f32[18,1152]{1,0:T(8,128)S(1)} %get-tuple-element.8.og), custom_call_target="tpu_custom_call" | custom-call | tf_op jit(solution)/shard_map/unpack/pallas_call | solution.py:404
Async XLA Ops:
  0.6 1.1 %copy-start = (bf16[1,1,256,1152]{3,2,1,0:T(8,128)(2,1)S(1)}, bf16[1,1,256,1152]{3,2,1,0:T(8,128)(2,1)}, u32[]{:S(2)}) copy-start(bf16[1,1,256,1152]{3,2,1,0:T(8,128)(2,1)} %param.5) | copy-start | bytes 1769476
  1.7 0.7 copy-start.1

commit v4 on v3

--- a/solution.py
+++ b/solution.py
@@ -34,13 +34,15 @@
     lat_hbm, cot_hbm, len_ref, inw_hbm, outw_hbm, mixed_o, glat_o, og_o = refs[:8]
     (
         latv, cotv, xs, xr, ms, gs, inw, inwT, outw, qkvT, w32s, attT, cp, gaT, gpT, glatT, paT, pc,
-        zs, zr, ogs, ogr, amask,
-    ) = refs[8:31]
+        amask,
+    ) = refs[8:27]
     (
         wsem, lsem, ssem, rsem, psem_s, psem_r, gsem_s, gsem_r, hsem_s, hsem_r,
         zsem_s, zsem_r, bsem_s, bsem_r,
-    ) = refs[31:45]
-    csp, crp, gsp, grp, gop, hsp, hrp = (refs[45 + NP * i : 45 + NP * i + NP] for i in range(7))
+    ) = refs[27:41]
+    csp, crp, gsp, grp, gop, hsp, hrp, zsp, zrp, ogsp, ogrp = (
+        refs[41 + NP * i : 41 + NP * i + NP] for i in range(11)
+    )
     x = lax.axis_index("dp")
     me = lax.axis_index("seq")
     z, y, c = me // (YS * CS), me // CS % YS, me % CS
@@ -139,29 +141,38 @@
     arrived(0, xs, xr)
     xp = dot(to_patch, xr[...].reshape(256, INNER)).astype(BF16)
 
-    @pl.loop(0, 6)
-    def _(n):
-        out = dot(inwT[pl.ds(pl.multiple_of(n * 576, 16), 576), :], xp, NT)
-        for i in range(8):
-            qkvT[n * 8 + i] = out[HD * i : HD * i + HD].astype(BF16)
+    @pl.loop(0, 2)
+    def _(n):
+        out = dot(inwT[pl.ds(pl.multiple_of(n * 1728, 16), 1728), :], xp, NT)
+        for i in range(24):
+            qkvT[n * 24 + i] = out[HD * i : HD * i + HD].astype(BF16)
 
 
     def lanes(i):
         return slice(128 * i, 128 * i + 128)
 
+    def diagonal(parts):
+        zero = jnp.zeros((128, 128), BF16)
+        top = jnp.concatenate([parts[0], zero], axis=1)
+        return jnp.concatenate([top, jnp.concatenate([zero, parts[1]], axis=1)], axis=0)
+
+    def group_rows(n, base=0):
+        return pl.ds(pl.multiple_of(base + n * (GROUP * HD), 16), GROUP * HD)
+
     @pl.loop(0, HEADS // GROUP)
     def _(n):
-        for i in range(2):
-            outs = []
-            for t in range(GROUP):
-                h = n * GROUP + t
+        outs = []
+        for t in range(GROUP):
+            h = n * GROUP + t
+            parts = []
+            for i in range(2):
                 s = dot(qkvT[HEADS + h, :, lanes(i)], qkvT[h, :, lanes(i)], TN) + amask[...]
                 e = jnp.exp2((s - jnp.max(s, axis=0, keepdims=True)) * (SCALE * LOG2E))
                 w = e / jnp.sum(e, axis=0, keepdims=True)
                 w32s[i, h] = w
-                outs.append(dot(qkvT[2 * HEADS + h, :, lanes(i)], w.astype(BF16)))
-            rows = pl.ds(pl.multiple_of(n * (GROUP * HD), 16), GROUP * HD)
-            attT[rows, lanes(i)] = jnp.concatenate(outs, axis=0).astype(BF16)
+                parts.append(w.astype(BF16))
+            outs.append(dot(qkvT[2 * HEADS + h], diagonal(parts)))
+        attT[group_rows(n), :] = jnp.concatenate(outs, axis=0).astype(BF16)
 
     mate = seq(z, y, 1 - c)
     theirs = pl.ds(pl.multiple_of((1 - c) * 576, 16), 576)
@@ -207,16 +218,16 @@
     def blocks(p):
         cot_copies[p].wait()
         for k in range(3):
-            gsp[p][k] = block((x + k + 1) % XS, COLS[p]).astype(BF16)
+            gsp[p][k] = block((x + k + 1 + p) % XS, COLS[p]).astype(BF16)
             first(k, p).start()
-        gop[p][...] = block(x, COLS[p])
+        gop[p][...] = block((x + p) % XS, COLS[p])
 
     cot_part(0)
     att_f = dot(to_frame, attT[...], NT).astype(BF16)
+    att_copy.wait()
+    blocks(0)
     ms[...] = dot(att_f, outw[...]).astype(BF16).reshape(SEQ, 4, INNER)
-    att_copy.wait()
     keep(1, ms, mixed_o).start()
-    blocks(0)
     cot_part(1)
     batch(1, ms, mixed_o, 0)
     blocks(1)
@@ -242,98 +253,106 @@
         for k in range(3):
             second(k, p).start()
 
-    root = seq(4 * c + x, y, c)
-    z_copy = pltpu.make_async_remote_copy(
-        src_ref=zs, dst_ref=zr.at[z], send_sem=zsem_s, recv_sem=zsem_r,
-        device_id=(x, root), device_id_type=MESH,
-    )
-
-    def second_sum():
-        for p in range(NP):
-            total = hsp[p][y].astype(F32)
-            for k in range(3):
-                second(k, p).wait()
-                total = total + hrp[p][k].astype(F32)
-            zs[:, COLS[p]] = total.astype(BF16)
-
-        @pl.when(root != me)
+    roots = [seq(4 * c + (x + p) % XS, y, c) for p in range(NP)]
+    def z_copy(p):
+        return pltpu.make_async_remote_copy(
+            src_ref=zsp[p], dst_ref=zrp[p].at[z], send_sem=zsem_s.at[p], recv_sem=zsem_r.at[p],
+            device_id=(x, roots[p]), device_id_type=MESH,
+        )
+
+    def second_sum(p):
+        total = hsp[p][y].astype(F32)
+        for k in range(3):
+            second(k, p).wait()
+            total = total + hrp[p][k].astype(F32)
+        zsp[p][...] = total.astype(BF16)
+
+        @pl.when(roots[p] != me)
         def _():
-            z_copy.start()
-
-        @pl.when(root == me)
+            z_copy(p).start()
+
+        @pl.when(roots[p] == me)
         def _():
-            zr[z] = zs[...]
-
-    def b_copy(k):
+            zrp[p][z] = zsp[p][...]
+
+    def b_copy(k, p):
         dx, dc = OTHERS[k]
         return pltpu.make_async_remote_copy(
-            src_ref=ogs.at[(c + dc) % CS], dst_ref=ogr, send_sem=bsem_s.at[k], recv_sem=bsem_r,
+            src_ref=ogsp[p].at[(c + dc) % CS], dst_ref=ogrp[p], send_sem=bsem_s.at[p, k], recv_sem=bsem_r.at[p],
             device_id=((x + dx) % XS, seq(z, y, (c + dc) % CS)), device_id_type=MESH,
         )
 
-    def z_sum():
-        @pl.when(root == me)
+    def z_sum(p):
+        @pl.when(roots[p] == me)
         def _():
-            part = zr.at[pl.ds(0, ZS - 1)]
-            pltpu.make_async_copy(part, part, zsem_r).wait()
-            total = zr[0].astype(F32)
+            part = zrp[p].at[pl.ds(0, ZS - 1)]
+            pltpu.make_async_copy(part, part, zsem_r.at[p]).wait()
+            total = zrp[p][0].astype(F32)
             for k in range(1, ZS):
-                total = total + zr[k].astype(F32)
-            ogs[0] = total[:18].astype(ogs.dtype)
-            ogs[1] = total[18:].astype(ogs.dtype)
+                total = total + zrp[p][k].astype(F32)
+            ogsp[p][0] = total[:18].astype(BF16)
+            ogsp[p][1] = total[18:].astype(BF16)
             for k in range(len(OTHERS)):
-                b_copy(k).start()
-
-    def last():
-        @pl.when(root == me)
+                b_copy(k, p).start()
+
+    def last(p):
+        @pl.when(roots[p] == me)
         def _():
-            og_o[...] = ogs[c].astype(F32)
+            og_o[:, COLS[p]] = ogsp[p][c].astype(F32)
             for k in range(len(OTHERS)):
-                b_copy(k).wait_send()
-
-        @pl.when(root != me)
+                b_copy(k, p).wait_send()
+
+        @pl.when(roots[p] != me)
         def _():
-            z_copy.wait_send()
-            b_copy(0).wait_recv()
-            og_o[...] = ogr[...].astype(F32)
+            z_copy(p).wait_send()
+            b_copy(0, p).wait_recv()
+            og_o[:, COLS[p]] = ogrp[p][...].astype(F32)
 
     def backward(n):
-        rows = [
-            pl.ds(pl.multiple_of(INNER * t + n * (GROUP * HD), 16), GROUP * HD) for t in range(3)
-        ]
-        for i in range(2):
-            outs = ([], [], [])
-            for t in range(GROUP):
-                h = n * GROUP + t
-                q, k, v = (qkvT[HEADS * u + h, :, lanes(i)] for u in range(3))
-                g = gaT[h, :, lanes(i)]
+        outs = ([], [], [])
+        for t in range(GROUP):
+            h = n * GROUP + t
+            ws, ds = [], []
+            for i in range(2):
                 w = w32s[i, h]
-                dw = dot(v, g, TN)
-                ds = (w * (dw - jnp.sum(w * dw, axis=0, keepdims=True)) * SCALE).astype(BF16)
-                outs[0].append(dot(k, ds))
-                outs[1].append(dot(q, ds, NT))
-                outs[2].append(dot(g, w.astype(BF16), NT))
-            for u in range(3):
-                gpT[rows[u], lanes(i)] = jnp.concatenate(outs[u], axis=0).astype(BF16)
+                dw = dot(qkvT[2 * HEADS + h, :, lanes(i)], gaT[h, :, lanes(i)], TN)
+                ds.append((w * (dw - jnp.sum(w * dw, axis=0, keepdims=True)) * SCALE).astype(BF16))
+                ws.append(w.astype(BF16))
+            ds = diagonal(ds)
+            outs[0].append(dot(qkvT[HEADS + h], ds))
+            outs[1].append(dot(qkvT[h], ds, NT))
+            outs[2].append(dot(gaT[h], diagonal(ws), NT))
+        for u in range(3):
+            gpT[group_rows(n, INNER * u), :] = jnp.concatenate(outs[u], axis=0).astype(BF16)
+    @pl.loop(0, 2)
+    def _(n):
+        backward(n)
         batch(1, ms, mixed_o, n + 3)
 
-    pl.loop(0, HEADS // GROUP)(backward)
     first_sum(0)
+    @pl.loop(2, 4)
+    def _(n):
+        backward(n)
+        batch(1, ms, mixed_o, n + 3)
+
     first_sum(1)
 
-    @pl.loop(0, 2)
-    def _(n):
-        rows = pl.ds(pl.multiple_of(n * 576, 16), 576)
-        glatT[rows, :] = dot(inw[rows, :], gpT[...]).astype(BF16)
-
+    glatT[...] = dot(inw[...], gpT[...]).astype(BF16)
+
+    gs[...] = dot(to_frame, glatT[...], NT).astype(BF16).reshape(SEQ, 4, INNER)
     first_sum(2)
-    gs[...] = dot(to_frame, glatT[...], NT).astype(BF16).reshape(SEQ, 4, INNER)
+
+    keep(2, gs, glat_o).start()
     batch(2, gs, glat_o, 0, 18)
-    second_sum()
-    batch(2, gs, glat_o, 18 // BATCH, SEQ - 1 - 18)
-    keep(2, gs, glat_o).start()
-    z_sum()
-    last()
+    second_sum(0)
+    second_sum(1)
+    batch(2, gs, glat_o, 18 // BATCH, 9)
+    second_sum(2)
+    batch(2, gs, glat_o, (18 + 9) // BATCH, SEQ - 1 - 18 - 9)
+    for p in range(NP):
+        z_sum(p)
+    for p in range(NP):
+        last(p)
     sent(0, xs)
     for p in range(NP):
         sent(3 + p, csp[p])
@@ -380,20 +399,20 @@
             pltpu.VMEM((INNER, 256), BF16),
             pltpu.VMEM((576, 256), BF16),
             pltpu.VMEM(tok, BF16),
-            pltpu.VMEM((36, INNER), BF16),
-            pltpu.VMEM((ZS, 36, INNER), BF16),
-            pltpu.VMEM((2, 18, INNER), BF16),
-            pltpu.VMEM((18, INNER), BF16),
             pltpu.VMEM((128, 128), F32),
             dma((4,)), dma((3 + NP,)), dma((3 + NP, 1)), dma((3 + NP,)), dma((1 + NP,)), dma((1 + NP,)),
-            dma((NP, 3)), dma((NP, 3)), dma((NP, 3)), dma((NP, 3)), dma, dma,
-            dma((7,)), dma,
+            dma((NP, 3)), dma((NP, 3)), dma((NP, 3)), dma((NP, 3)), dma((NP,)), dma((NP,)),
+            dma((NP, 7)), dma((NP,)),
         ]
         + [pltpu.VMEM((SEQ, 4, w), BF16) for w in WIDTHS] * 2
         + [pltpu.VMEM((3, 144, w), BF16) for w in WIDTHS] * 2
         + [pltpu.VMEM((144, w), F32) for w in WIDTHS]
         + [pltpu.VMEM((4, 36, w), BF16) for w in WIDTHS]
-        + [pltpu.VMEM((3, 36, w), BF16) for w in WIDTHS],
+        + [pltpu.VMEM((3, 36, w), BF16) for w in WIDTHS]
+        + [pltpu.VMEM((36, w), BF16) for w in WIDTHS]
+        + [pltpu.VMEM((ZS, 36, w), BF16) for w in WIDTHS]
+        + [pltpu.VMEM((2, 18, w), BF16) for w in WIDTHS]
+        + [pltpu.VMEM((18, w), BF16) for w in WIDTHS],
         compiler_params=pltpu.CompilerParams(
             collective_id=0, has_side_effects=True, vmem_limit_bytes=52 << 20
         ),

time: 79.4 us -> 75.6 us (0.952)
  Pallas kernels: 76.9 us -> 73.1 us
    pallas_call x1, Pallas kernels: 75.7 us -> 71.9 us  [body(): pl.pallas_call(kernel, out_shape=[jax.ShapeDtypeStruct(msg, BF16), jax.Sh...]
where the time goes in v4:
time: 75.6 us; the launch traced here: 75.4 us
  Pallas kernels  73.1 us (97%)
  local copies, waits for them, and re-layouts  1.71 us (2%)
    pallas_call x1, Pallas kernels, body(): pl.pallas_call(kernel, out_shape=[jax.ShapeDtypeStruct(msg, BF16), jax.Sh...  71.9 us
    unnamed x4, local copies, waits for them, and re-layouts  1.71 us

profile of v4, /device:TPU:1, one launch (start us, length us, event | category | flops | bytes accessed | tf_op | source)
XLA Modules:
  0.0 75.4 jit_solution(12281121191368982492)
XLA Ops:
  0.6 0.0 copy-start
  0.6 1.1 %copy-done = bf16[1,1,256,1152]{3,2,1,0:T(8,128)(2,1)S(1)} copy-done((bf16[1,1,256,1152]{3,2,1,0:T(8,128)(2,1)S(1)}, bf16[1,1,256,1152]{3,2,1,0:T(8,128)(2,1)}, u32[]{:S(2)}) %copy-start) | copy-done | bytes 589848
  1.7 0.0 copy-start.1
  1.7 0.7 copy-done.1
  2.4 71.9 %sublayer.1 = (bf16[64,4,1152]{2,1,0:T(4,128)(2,1)S(1)}, bf16[64,4,1152]{2,1,0:T(4,128)(2,1)S(1)}, f32[18,1152]{1,0:T(8,128)S(1)}) custom-call(bf16[256,1152]{1,0:T(8,128)(2,1)S(1)} %bitcast.2, bf16[256,1152]{1,0:T(8,128)(2,1)} %bitcast.3, s32[1,4]{1,0:T(1,128)S(1)} %copy-done.1, bf16[1152,3456]{1,0:T(8,128)(2,1)} %refs_3_.1, bf16[1152,1152]{1,0:T(8,128)(2,1)} %refs_4_.1), custom_call_target="tpu_custom_call" | custom-call | tf_op jit(solution)/shard_map/sublayer/pallas_call | solution.py:378
  74.2 1.2 %unpack.1 = (bf16[1,1,256,1152]{3,2,1,0:T(8,128)(2,1)}, bf16[1,1,256,1152]{3,2,1,0:T(8,128)(2,1)}, f32[18,1152]{1,0:T(8,128)}) custom-call(bf16[64,4,1152]{2,1,0:T(4,128)(2,1)S(1)} %get-tuple-element.6.mixed, bf16[64,4,1152]{2,1,0:T(4,128)(2,1)S(1)} %get-tuple-element.7.glat, f32[18,1152]{1,0:T(8,128)S(1)} %get-tuple-element.8.og), custom_call_target="tpu_custom_call" | custom-call | tf_op jit(solution)/shard_map/unpack/pallas_call | solution.py:423
Async XLA Ops:
  0.6 1.1 %copy-start = (bf16[1,1,256,1152]{3,2,1,0:T(8,128)(2,1)S(1)}, bf16[1,1,256,1152]{3,2,1,0:T(8,128)(2,1)}, u32[]{:S(2)}) copy-start(bf16[1,1,256,1152]{3,2,1,0:T(8,128)(2,1)} %param.5) | copy-start | bytes 1769476
  1.7 0.7 copy-start.1

commit v5 on v4

--- a/solution.py
+++ b/solution.py
@@ -31,17 +31,17 @@
 
 
 def kernel(*refs):
-    lat_hbm, cot_hbm, len_ref, inw_hbm, outw_hbm, mixed_o, glat_o, og_o = refs[:8]
+    lat_hbm, cot_hbm, len_hbm, inw_hbm, outw_hbm, mixed_o, glat_o, og_hbm = refs[:8]
     (
         latv, cotv, xs, xr, ms, gs, inw, inwT, outw, qkvT, w32s, attT, cp, gaT, gpT, glatT, paT, pc,
-        amask,
-    ) = refs[8:27]
+        amask, og_o, len_ref,
+    ) = refs[8:29]
     (
         wsem, lsem, ssem, rsem, psem_s, psem_r, gsem_s, gsem_r, hsem_s, hsem_r,
         zsem_s, zsem_r, bsem_s, bsem_r,
-    ) = refs[27:41]
+    ) = refs[29:43]
     csp, crp, gsp, grp, gop, hsp, hrp, zsp, zrp, ogsp, ogrp = (
-        refs[41 + NP * i : 41 + NP * i + NP] for i in range(11)
+        refs[43 + NP * i : 43 + NP * i + NP] for i in range(11)
     )
     x = lax.axis_index("dp")
     me = lax.axis_index("seq")
@@ -52,7 +52,7 @@
 
     loads = [
         pltpu.make_async_copy(s, d, wsem.at[k])
-        for k, (s, d) in enumerate(((lat_hbm, latv), (cot_hbm, cotv), (inw_hbm, inw), (outw_hbm, outw)))
+        for k, (s, d) in enumerate(((lat_hbm, latv), (cot_hbm, cotv), (inw_hbm, inw), (outw_hbm, outw), (len_hbm, len_ref)))
     ]
     for t in loads:
         t.start()
@@ -80,7 +80,11 @@
         @pl.loop(0, size, unroll=9)
         def _(j):
             n = b * BATCH + j
-            d = peer(n % 8, 7 - n // 8)
+            if k == 2:
+                n = n + (n + 56) // 63
+                d = peer(n % 8, n // 8)
+            else:
+                d = peer(n % 8, 7 - n // 8)
             pltpu.make_async_remote_copy(
                 src_ref=src.at[d], dst_ref=dst.at[me], send_sem=ssem.at[k, sem], recv_sem=rsem.at[k],
                 device_id=(x, d), device_id_type=MESH,
@@ -112,6 +116,7 @@
     to_patch = (c_i == r_i % SEQ * 4 + r_i // SEQ).astype(BF16)
     to_frame = (r_i == c_i % SEQ * 4 + c_i // SEQ).astype(BF16)
 
+    loads[4].wait()
     ends = [len_ref[0, 0]]
     for i in range(1, 4):
         ends.append(ends[-1] + len_ref[0, i])
@@ -229,10 +234,10 @@
     ms[...] = dot(att_f, outw[...]).astype(BF16).reshape(SEQ, 4, INNER)
     keep(1, ms, mixed_o).start()
     cot_part(1)
-    batch(1, ms, mixed_o, 0)
+    batch(1, ms, mixed_o, 0, 2 * BATCH)
     blocks(1)
     cot_part(2)
-    batch(1, ms, mixed_o, 1)
+    batch(1, ms, mixed_o, 2)
 
     @pl.loop(0, 2)
     def _(n):
@@ -241,7 +246,7 @@
             gaT[n * 8 + i] = out[HD * i : HD * i + HD].astype(BF16)
 
     blocks(2)
-    batch(1, ms, mixed_o, 2)
+    batch(1, ms, mixed_o, 3)
 
     def first_sum(p):
         total = gop[p][...]
@@ -327,13 +332,13 @@
     @pl.loop(0, 2)
     def _(n):
         backward(n)
-        batch(1, ms, mixed_o, n + 3)
+        batch(1, ms, mixed_o, n + 4)
 
     first_sum(0)
     @pl.loop(2, 4)
     def _(n):
         backward(n)
-        batch(1, ms, mixed_o, n + 3)
+        pl.when(n == 2)(lambda: batch(1, ms, mixed_o, 6))
 
     first_sum(1)
 
@@ -343,16 +348,18 @@
     first_sum(2)
 
     keep(2, gs, glat_o).start()
-    batch(2, gs, glat_o, 0, 18)
+    batch(2, gs, glat_o, 0, 9)
     second_sum(0)
     second_sum(1)
-    batch(2, gs, glat_o, 18 // BATCH, 9)
+    batch(2, gs, glat_o, 9 // BATCH, 9)
     second_sum(2)
-    batch(2, gs, glat_o, (18 + 9) // BATCH, SEQ - 1 - 18 - 9)
+    batch(2, gs, glat_o, (9 + 9) // BATCH, SEQ - 1 - 9 - 9)
     for p in range(NP):
         z_sum(p)
     for p in range(NP):
         last(p)
+    og_copy = pltpu.make_async_copy(og_o, og_hbm, wsem.at[5])
+    og_copy.start()
     sent(0, xs)
     for p in range(NP):
         sent(3 + p, csp[p])
@@ -360,6 +367,7 @@
     sent(2, gs)
     arrived(1, ms, mixed_o)
     arrived(2, gs, glat_o)
+    og_copy.wait()
 
 
 def unpack(mixed, glat, og, mixed_o, glat_o, og_o):
@@ -382,8 +390,8 @@
             jax.ShapeDtypeStruct(msg, BF16),
             jax.ShapeDtypeStruct((18, INNER), F32),
         ],
-        in_specs=[hbm, hbm, pl.BlockSpec(memory_space=pltpu.SMEM), hbm, hbm],
-        out_specs=[hbm, hbm, vmem],
+        in_specs=[hbm] * 5,
+        out_specs=[hbm] * 3,
         scratch_shapes=[pltpu.VMEM(tok, BF16)] * 2
         + [pltpu.VMEM(msg, BF16)] * 4
         + [
@@ -400,7 +408,9 @@
             pltpu.VMEM((576, 256), BF16),
             pltpu.VMEM(tok, BF16),
             pltpu.VMEM((128, 128), F32),
-            dma((4,)), dma((3 + NP,)), dma((3 + NP, 1)), dma((3 + NP,)), dma((1 + NP,)), dma((1 + NP,)),
+            pltpu.VMEM((18, INNER), F32),
+            pltpu.SMEM((1, 4), jnp.int32),
+            dma((6,)), dma((3 + NP,)), dma((3 + NP, 1)), dma((3 + NP,)), dma((1 + NP,)), dma((1 + NP,)),
             dma((NP, 3)), dma((NP, 3)), dma((NP, 3)), dma((NP, 3)), dma((NP,)), dma((NP,)),
             dma((NP, 7)), dma((NP,)),
         ]

time: 75.6 us -> 75.1 us (level)
  no operation moved by 1% of the time
where the time goes in v5:
time: 75.1 us; the launch traced here: 74.9 us
  Pallas kernels  72.6 us (97%)
  local copies, waits for them, and re-layouts  1.71 us (2%)
    pallas_call x1, Pallas kernels, body(): pl.pallas_call(kernel, out_shape=[jax.ShapeDtypeStruct(msg, BF16), jax.Sh...  71.4 us
    unnamed x4, local copies, waits for them, and re-layouts  1.71 us

profile of v5, /device:TPU:1, one launch (start us, length us, event | category | flops | bytes accessed | tf_op | source)
XLA Modules:
  0.0 74.9 jit_solution(7638794468923035721)
XLA Ops:
  0.6 0.0 copy-start
  0.6 1.1 %copy-done = bf16[1,1,256,1152]{3,2,1,0:T(8,128)(2,1)S(1)} copy-done((bf16[1,1,256,1152]{3,2,1,0:T(8,128)(2,1)S(1)}, bf16[1,1,256,1152]{3,2,1,0:T(8,128)(2,1)}, u32[]{:S(2)}) %copy-start) | copy-done | bytes 589848
  1.7 0.0 copy-start.1
  1.7 0.7 copy-done.1
  2.4 71.4 %sublayer.1 = (bf16[64,4,1152]{2,1,0:T(4,128)(2,1)S(1)}, bf16[64,4,1152]{2,1,0:T(4,128)(2,1)S(1)}, f32[18,1152]{1,0:T(8,128)S(1)}) custom-call(bf16[256,1152]{1,0:T(8,128)(2,1)S(1)} %bitcast.2, bf16[256,1152]{1,0:T(8,128)(2,1)} %bitcast.3, s32[1,4]{1,0:T(1,128)S(1)} %copy-done.1, bf16[1152,3456]{1,0:T(8,128)(2,1)} %refs_3_.1, bf16[1152,1152]{1,0:T(8,128)(2,1)} %refs_4_.1), custom_call_target="tpu_custom_call" | custom-call | tf_op jit(solution)/shard_map/sublayer/pallas_call | solution.py:386
  73.8 1.2 %unpack.1 = (bf16[1,1,256,1152]{3,2,1,0:T(8,128)(2,1)}, bf16[1,1,256,1152]{3,2,1,0:T(8,128)(2,1)}, f32[18,1152]{1,0:T(8,128)}) custom-call(bf16[64,4,1152]{2,1,0:T(4,128)(2,1)S(1)} %get-tuple-element.6.mixed, bf16[64,4,1152]{2,1,0:T(4,128)(2,1)S(1)} %get-tuple-element.7.glat, f32[18,1152]{1,0:T(8,128)S(1)} %get-tuple-element.8.og), custom_call_target="tpu_custom_call" | custom-call | tf_op jit(solution)/shard_map/unpack/pallas_call | solution.py:433
Async XLA Ops:
  0.6 1.1 %copy-start = (bf16[1,1,256,1152]{3,2,1,0:T(8,128)(2,1)S(1)}, bf16[1,1,256,1152]{3,2,1,0:T(8,128)(2,1)}, u32[]{:S(2)}) copy-start(bf16[1,1,256,1152]{3,2,1,0:T(8,128)(2,1)} %param.5) | copy-start | bytes 1769476
  1.7 0.7 copy-start.1
